TPU v7x, 32 devices: a whole 2x2x4 slice. The times are simulated.
32 devices in a mesh: view: 4 (over y, x), brick: 8 (over z, core).
Axes of the slice: x: 2, y: 2, z: 4, core: 2. Of those that a mesh axis runs over, the one named last changes fastest.
Arguments:
- view_stacks: float32 [4, 128, 256, 256], P('view', 'brick'), may hold values from 0.2 to 5
- point_spread: float32 [4, 128, 256, 256], P('view', 'brick'), may hold values from 0 to 2, as said below
- weights_depth: float32 [4, 128, 128], P('view'), may hold values from 0 to 2, as said below
- weights_rows: float32 [4, 256, 256], P('view'), may hold values from 0 to 2, as said below
- weights_cols: float32 [4, 256, 256], P('view'), may hold values from 0 to 2, as said below
- depth_start: int32 [4, 256, 256], P('view'), may hold values from 0 to 63
- depth_stop: int32 [4, 256, 256], P('view'), may hold values from 65 to 128
Outputs:
- joined_brick: float32 [128, 256, 256], P('brick')
- deconvolved: float32 [128, 256, 256], P('brick')
Inputs may be any that keep to these rules, and one draw needn't show every extreme that they name: `point_spread`: nonnegative. `weights_depth`: nonnegative. `weights_rows`: nonnegative. `weights_cols`: nonnegative.
All inputs are finite; a program needn't handle non-finite values.
Results may differ from a plain program's by a relative error of at most 0.00012.
Values sent between devices are 32-bit elements; how exact they have to be, the bound alone decides.
A program may use at most 192 MiB of HBM per device.

v0:
```python
import math

import jax
import jax.numpy as jnp
from jax import lax
from jax.sharding import PartitionSpec as P

highest = lax.Precision.HIGHEST
einsum_forms = ("kyx,kj->jyx", "zkx,kj->zjx", "zyk,kj->zyj")


def dft_tables(length):
    counter = jnp.arange(length, dtype=jnp.int32)
    product = counter[:, None] * counter[None, :] % length
    angles = product.astype(jnp.float32) * (2.0 * math.pi / length)
    return (jnp.cos(angles), jnp.sin(angles))


def along_axis(values_in, table, axis_index):
    return jnp.einsum(einsum_forms[axis_index], values_in, table, precision=highest)


def forward_axis(real_part, imag_part, axis_index):
    cosine, sine = dft_tables(real_part.shape[axis_index])
    if imag_part is None:
        return (along_axis(real_part, cosine, axis_index), -along_axis(real_part, sine, axis_index))
    new_real = along_axis(real_part, cosine, axis_index) + along_axis(imag_part, sine, axis_index)
    new_imag = along_axis(imag_part, cosine, axis_index) - along_axis(real_part, sine, axis_index)
    return (new_real, new_imag)


def inverse_axis(real_part, imag_part, axis_index, real_only):
    length = real_part.shape[axis_index]
    cosine, sine = dft_tables(length)
    scale = 1.0 / length
    new_real = (
        along_axis(real_part, cosine, axis_index) - along_axis(imag_part, sine, axis_index)
    ) * scale
    if real_only:
        return new_real
    new_imag = (
        along_axis(imag_part, cosine, axis_index) + along_axis(real_part, sine, axis_index)
    ) * scale
    return (new_real, new_imag)


def resample_view(source, depth_map, row_map, col_map):
    across = jnp.einsum("zyx,ax->zya", source, col_map, precision=highest)
    across = jnp.einsum("zyx,by->zbx", across, row_map, precision=highest)
    mixed = jnp.einsum(
        "zyx,cz->cyx",
        lax.all_to_all(across, "brick", split_axis=1, concat_axis=0, tiled=True),
        depth_map,
        precision=highest,
    )
    return lax.all_to_all(mixed, "brick", split_axis=0, concat_axis=1, tiled=True)


def forward_transform(grid_values):
    real_part, imag_part = forward_axis(grid_values, None, 2)
    real_part, imag_part = forward_axis(real_part, imag_part, 1)
    depth_real, depth_imag = forward_axis(
        lax.all_to_all(real_part, "brick", split_axis=1, concat_axis=0, tiled=True),
        lax.all_to_all(imag_part, "brick", split_axis=1, concat_axis=0, tiled=True),
        0,
    )
    return (
        lax.all_to_all(depth_real, "brick", split_axis=0, concat_axis=1, tiled=True),
        lax.all_to_all(depth_imag, "brick", split_axis=0, concat_axis=1, tiled=True),
    )


def inverse_transform(real_part, imag_part):
    real_part, imag_part = (
        lax.all_to_all(real_part, "brick", split_axis=1, concat_axis=0, tiled=True),
        lax.all_to_all(imag_part, "brick", split_axis=1, concat_axis=0, tiled=True),
    )
    real_part, imag_part = inverse_axis(real_part, imag_part, 0, False)
    real_part, imag_part = inverse_axis(
        lax.all_to_all(real_part, "brick", split_axis=0, concat_axis=1, tiled=True),
        lax.all_to_all(imag_part, "brick", split_axis=0, concat_axis=1, tiled=True),
        1,
        False,
    )
    return inverse_axis(real_part, imag_part, 2, True)


def per_device(
    view_stacks, point_spread, weights_depth, weights_rows, weights_cols, depth_start, depth_stop
):
    resampled = resample_view(view_stacks[0], weights_depth[0], weights_rows[0], weights_cols[0])
    planes_here = resampled.shape[0]
    depth_index = lax.axis_index("brick") * planes_here + jnp.arange(planes_here, dtype=jnp.int32)
    depth_grid = depth_index[:, None, None]
    covered = jnp.logical_and(
        depth_grid >= depth_start[0][None], depth_grid < depth_stop[0][None]
    ).astype(jnp.float32)
    view_weight = 0.05 + covered * (1.0 + jnp.log(1.0 + resampled * resampled))
    weighted = view_weight * resampled
    total_signal, total_weight = lax.psum((weighted, view_weight), "view")
    joined_brick = total_signal / total_weight
    otf_real, otf_imag = forward_transform(point_spread[0])
    joined_real, joined_imag = forward_transform(joined_brick)
    blurred = inverse_transform(
        joined_real * otf_real - joined_imag * otf_imag,
        joined_real * otf_imag + joined_imag * otf_real,
    )
    ratio = resampled / blurred
    ratio_real, ratio_imag = forward_transform(ratio)
    correction = inverse_transform(
        ratio_real * otf_real + ratio_imag * otf_imag, ratio_imag * otf_real - ratio_real * otf_imag
    )
    correction_total = lax.psum(view_weight * correction, "view")
    deconvolved = joined_brick * correction_total / total_weight
    return (joined_brick, deconvolved)


def solution(mesh):
    return jax.shard_map(
        per_device,
        mesh=mesh,
        in_specs=(
            P("view", "brick", None, None),
            P("view", "brick", None, None),
            P("view", None, None),
            P("view", None, None),
            P("view", None, None),
            P("view", None, None),
            P("view", None, None),
        ),
        out_specs=(P("brick", None, None), P("brick", None, None)),
        check_vma=False,
    )
```

profile of v0, /device:TPU:0, one launch (start us, length us, event | category | flops | bytes accessed | tf_op | source)
XLA Modules:
  0.0 2484.0 jit_solution(6937730432940994262)
XLA Ops:
  8.1 5.7 fusion.25
  13.8 5.0 convolution_bitcast_fusion
  18.8 5.4 copy.144
  24.3 6.3 all-to-all-start
  30.6 10.7 fusion.16
  41.4 7.6 fusion.18
  49.0 8.1 fusion.10
  57.1 7.6 add_bitcast_fusion.1
  69.3 55.4 %all-to-all-done = f32[16,256,256]{2,0,1:T(8,128)} async-done(((f32[16,256,256]{2,0,1:T(8,128)}), f32[16,256,256]{2,0,1:T(8,128)}, u32[]{:S(2)}, u32[]{:S(2)}) %all-to-all-start) | async-done | bytes 4194336 | tf_op jit(solution)/shard_map/all_to_all | solution.py:52
  133.9 9.4 fusion.47
  143.3 5.4 copy.148
  148.7 74.5 %all-to-all-done.5 = f32[16,256,256]{2,0,1:T(8,128)} async-done(((f32[16,256,256]{2,0,1:T(8,128)}), f32[16,256,256]{2,0,1:T(8,128)}, u32[]{:S(2)}, u32[]{:S(2)}) %all-to-all-start.5) | async-done | bytes 4194336 | tf_op jit(solution)/shard_map/all_to_all | solution.py:63
  227.9 11.0 fusion.8
  238.9 7.6 subtract_bitcast_fusion.1
  251.0 70.8 %all-to-all-done.1 = f32[128,32,256]{2,1,0:T(8,128)} async-done(((f32[128,32,256]{2,1,0:T(8,128)}), f32[128,32,256]{2,1,0:T(8,128)}, u32[]{:S(2)}, u32[]{:S(2)}) %all-to-all-start.1) | async-done | bytes 4194336 | tf_op jit(solution)/shard_map/all_to_all | solution.py:56
  329.1 5.5 fusion.24
  334.6 4.9 copy.166
  339.5 80.9 %all-to-all-done.6 = f32[16,256,256]{2,0,1:T(8,128)} async-done(((f32[16,256,256]{2,0,1:T(8,128)}), f32[16,256,256]{2,0,1:T(8,128)}, u32[]{:S(2)}, u32[]{:S(2)}) %all-to-all-start.6) | async-done | bytes 4194336 | tf_op jit(solution)/shard_map/all_to_all | solution.py:64
  440.6 68.1 %all-reduce.6.cloned.1.call-done = (f32[16,256,256]{2,1,0:T(8,128)}, f32[16,256,256]{2,1,0:T(8,128)}) async-done(((f32[16,256,256]{2,1,0:T(8,128)}, f32[16,256,256]{2,1,0:T(8,128)}), (f32[16,256,256]{2,1,0:T(8,128)}, f32[16,256,256]{2,1,0:T(8,128)})) %all-reduce.6.cloned.1.call-update) | async-done | bytes 8388624 | tf_op jit(solution)/shard_map/psum | solution.py:100
  521.8 5.6 fusion.111
  527.4 4.9 add_bitcast_fusion.2
  541.6 7.5 fusion.87
  558.1 77.5 %all-to-all-done.2 = f32[16,256,256]{2,0,1:T(8,128)} async-done(((f32[16,256,256]{2,0,1:T(8,128)}), f32[16,256,256]{2,0,1:T(8,128)}, u32[]{:S(2)}, u32[]{:S(2)}) %all-to-all-start.2) | async-done | bytes 4194336 | tf_op jit(solution)/shard_map/all_to_all | solution.py:63
  640.4 6.0 fusion.185
  654.9 79.5 %all-to-all-done.3 = f32[16,256,256]{2,0,1:T(8,128)} async-done(((f32[16,256,256]{2,0,1:T(8,128)}), f32[16,256,256]{2,0,1:T(8,128)}, u32[]{:S(2)}, u32[]{:S(2)}) %all-to-all-start.3) | async-done | bytes 4194336 | tf_op jit(solution)/shard_map/all_to_all | solution.py:64
  734.4 5.0 all-to-all-start.7
  759.1 74.3 %all-to-all-done.7 = f32[128,32,256]{2,1,0:T(8,128)} async-done(((f32[128,32,256]{2,1,0:T(8,128)}), f32[128,32,256]{2,1,0:T(8,128)}, u32[]{:S(2)}, u32[]{:S(2)}) %all-to-all-start.7) | async-done | bytes 4194336 | tf_op jit(solution)/shard_map/all_to_all | solution.py:68
  838.1 6.0 fusion.187
  852.7 79.4 %all-to-all-done.8 = f32[128,32,256]{2,1,0:T(8,128)} async-done(((f32[128,32,256]{2,1,0:T(8,128)}), f32[128,32,256]{2,1,0:T(8,128)}, u32[]{:S(2)}, u32[]{:S(2)}) %all-to-all-start.8) | async-done | bytes 4194336 | tf_op jit(solution)/shard_map/all_to_all | solution.py:69
  932.1 97.9 %all_to_all.342 = f32[128,32,256]{2,1,0:T(8,128)S(1)} all-to-all(f32[128,32,256]{2,1,0:T(8,128)} %copy.158), channel_id=1, replica_groups=mesh['view'=4,'brick'=8] {'brick'}, dimensions={0} | all-to-all | bytes 8388608 | tf_op jit(solution)/shard_map/all_to_all | solution.py:68
  1030.0 10.5 multiply_subtract_fusion.1
  1059.1 87.0 %all-to-all-done.11 = f32[16,256,256]{2,0,1:T(8,128)} async-done(((f32[16,256,256]{2,0,1:T(8,128)}), f32[16,256,256]{2,0,1:T(8,128)}, u32[]{:S(2)}, u32[]{:S(2)}) %all-to-all-start.11) | async-done | bytes 4194336 | tf_op jit(solution)/shard_map/all_to_all | solution.py:76
  1146.0 5.0 all-to-all-start.10
  1155.8 89.2 %all-to-all-done.10 = f32[16,256,256]{2,0,1:T(8,128)} async-done(((f32[16,256,256]{2,0,1:T(8,128)}), f32[16,256,256]{2,0,1:T(8,128)}, u32[]{:S(2)}, u32[]{:S(2)}) %all-to-all-start.10) | async-done | bytes 4194336 | tf_op jit(solution)/shard_map/all_to_all | solution.py:75
  1266.1 6.0 fusion.179
  1280.8 79.3 %all-to-all-done.13 = f32[128,32,256]{2,1,0:T(8,128)} async-done(((f32[128,32,256]{2,1,0:T(8,128)}), f32[128,32,256]{2,1,0:T(8,128)}, u32[]{:S(2)}, u32[]{:S(2)}) %all-to-all-start.13) | async-done | bytes 4194336 | tf_op jit(solution)/shard_map/all_to_all | solution.py:81
  1367.1 7.1 fusion.99
  1374.2 7.5 fusion.82
  1381.7 76.9 %all-to-all-done.12 = f32[128,32,256]{2,1,0:T(8,128)} async-done(((f32[128,32,256]{2,1,0:T(8,128)}), f32[128,32,256]{2,1,0:T(8,128)}, u32[]{:S(2)}, u32[]{:S(2)}) %all-to-all-start.12) | async-done | bytes 4194336 | tf_op jit(solution)/shard_map/all_to_all | solution.py:80
  1465.9 5.1 fusion.113
  1475.9 5.0 bitcast_divide_fusion
  1508.9 7.5 fusion.77
  1525.6 77.4 %all-to-all-done.14 = f32[16,256,256]{2,0,1:T(8,128)} async-done(((f32[16,256,256]{2,0,1:T(8,128)}), f32[16,256,256]{2,0,1:T(8,128)}, u32[]{:S(2)}, u32[]{:S(2)}) %all-to-all-start.14) | async-done | bytes 4194336 | tf_op jit(solution)/shard_map/all_to_all | solution.py:63
  1612.5 89.2 %all-to-all-done.15 = f32[16,256,256]{2,0,1:T(8,128)} async-done(((f32[16,256,256]{2,0,1:T(8,128)}), f32[16,256,256]{2,0,1:T(8,128)}, u32[]{:S(2)}, u32[]{:S(2)}) %all-to-all-start.15) | async-done | bytes 4194336 | tf_op jit(solution)/shard_map/all_to_all | solution.py:64
  1717.1 5.0 all-to-all-start.17
  1722.1 6.0 fusion.175
  1736.6 79.5 %all-to-all-done.17 = f32[128,32,256]{2,1,0:T(8,128)} async-done(((f32[128,32,256]{2,1,0:T(8,128)}), f32[128,32,256]{2,1,0:T(8,128)}, u32[]{:S(2)}, u32[]{:S(2)}) %all-to-all-start.17) | async-done | bytes 4194336 | tf_op jit(solution)/shard_map/all_to_all | solution.py:69
  1816.1 97.8 %all_to_all.343 = f32[128,32,256]{2,1,0:T(8,128)S(1)} all-to-all(f32[128,32,256]{2,1,0:T(8,128)} %copy.200), channel_id=1, replica_groups=mesh['view'=4,'brick'=8] {'brick'}, dimensions={0} | all-to-all | bytes 8388608 | tf_op jit(solution)/shard_map/all_to_all | solution.py:68
  1913.9 10.6 multiply_add_fusion
  1942.9 87.1 %all-to-all-done.19 = f32[16,256,256]{2,0,1:T(8,128)} async-done(((f32[16,256,256]{2,0,1:T(8,128)}), f32[16,256,256]{2,0,1:T(8,128)}, u32[]{:S(2)}, u32[]{:S(2)}) %all-to-all-start.19) | async-done | bytes 4194336 | tf_op jit(solution)/shard_map/all_to_all | solution.py:76
  2034.8 4.9 copy.209
  2039.6 89.1 %all-to-all-done.18 = f32[16,256,256]{2,0,1:T(8,128)} async-done(((f32[16,256,256]{2,0,1:T(8,128)}), f32[16,256,256]{2,0,1:T(8,128)}, u32[]{:S(2)}, u32[]{:S(2)}) %all-to-all-start.18) | async-done | bytes 4194336 | tf_op jit(solution)/shard_map/all_to_all | solution.py:75
  2144.9 5.0 all-to-all-start.21
  2150.0 6.0 fusion.171
  2164.7 79.2 %all-to-all-done.21 = f32[128,32,256]{2,1,0:T(8,128)} async-done(((f32[128,32,256]{2,1,0:T(8,128)}), f32[128,32,256]{2,1,0:T(8,128)}, u32[]{:S(2)}, u32[]{:S(2)}) %all-to-all-start.21) | async-done | bytes 4194336 | tf_op jit(solution)/shard_map/all_to_all | solution.py:81
  2251.1 7.1 fusion.96
  2258.2 7.2 fusion.75
  2265.4 77.1 %all-to-all-done.20 = f32[128,32,256]{2,1,0:T(8,128)} async-done(((f32[128,32,256]{2,1,0:T(8,128)}), f32[128,32,256]{2,1,0:T(8,128)}, u32[]{:S(2)}, u32[]{:S(2)}) %all-to-all-start.20) | async-done | bytes 4194336 | tf_op jit(solution)/shard_map/all_to_all | solution.py:80
  2345.0 5.1 fusion.73
  2350.1 5.1 fusion.117
  2355.2 4.8 fusion
  2360.1 6.6 multiply_multiply_fusion
  2366.7 102.6 %all-reduce.4.cloned.1.call-done = f32[16,256,256]{2,1,0:T(8,128)} async-done(((f32[16,256,256]{2,1,0:T(8,128)}), f32[16,256,256]{2,1,0:T(8,128)}) %all-reduce.4.cloned.1.call-update) | async-done | bytes 4194320 | tf_op jit(solution)/shard_map/psum | solution.py:113
  2469.4 7.6 multiply_divide_fusion
  (163 shorter events, 329.1 us)
Async XLA Ops:
  7.2 1.0 copy-start
  7.2 6.6 copy-start.35
  24.3 100.4 %all-to-all-start = ((f32[16,256,256]{2,0,1:T(8,128)}), f32[16,256,256]{2,0,1:T(8,128)}, u32[]{:S(2)}, u32[]{:S(2)}) async-start(f32[16,256,256]{2,0,1:T(8,128)} %copy.144), calls=%async_computation | async-start | bytes 8388608 | tf_op jit(solution)/shard_map/all_to_all | solution.py:52
  30.6 10.8 copy-start.34
  41.3 15.7 copy-start.27
  49.0 8.1 copy-start.3
  124.7 98.6 %all-to-all-start.5 = ((f32[16,256,256]{2,0,1:T(8,128)}), f32[16,256,256]{2,0,1:T(8,128)}, u32[]{:S(2)}, u32[]{:S(2)}) async-start(f32[16,256,256]{2,0,1:T(8,128)} %copy.165), calls=%async_computation.5 | async-start | bytes 8388608 | tf_op jit(solution)/shard_map/all_to_all | solution.py:63
  129.3 4.6 copy-start.38
  223.3 98.6 %all-to-all-start.1 = ((f32[128,32,256]{2,1,0:T(8,128)}), f32[128,32,256]{2,1,0:T(8,128)}, u32[]{:S(2)}, u32[]{:S(2)}) async-start(f32[128,32,256]{2,1,0:T(8,128)} %copy.148), calls=%async_computation.1 | async-start | bytes 8388608 | tf_op jit(solution)/shard_map/all_to_all | solution.py:56
  227.8 11.0 copy-start.4
  321.8 98.6 %all-to-all-start.6 = ((f32[16,256,256]{2,0,1:T(8,128)}), f32[16,256,256]{2,0,1:T(8,128)}, u32[]{:S(2)}, u32[]{:S(2)}) async-start(f32[16,256,256]{2,0,1:T(8,128)} %copy.171), calls=%async_computation.6 | async-start | bytes 8388608 | tf_op jit(solution)/shard_map/all_to_all | solution.py:64
  326.4 182.2 %all-reduce.6.cloned.1.call-start = ((), (), s32[]{:S(2)}) async-start(), calls=%async_computation.23 | async-start | bytes 16777216 | tf_op jit(solution)/shard_map/psum | solution.py:100
  326.5 2.6 copy-start.36
  326.5 2.6 copy-start.37
  329.1 5.5 copy-start.10
  423.3 4.0 copy-start.13
  423.3 4.0 copy-start.12
  436.0 100.8 %all-to-all-start.9 = ((f32[128,32,256]{2,1,0:T(8,128)}), f32[128,32,256]{2,1,0:T(8,128)}, u32[]{:S(2)}, u32[]{:S(2)}) async-start(f32[128,32,256]{2,1,0:T(8,128)} %copy.175), calls=%async_computation.9 | async-start | bytes 8388608 | tf_op jit(solution)/shard_map/all_to_all | solution.py:69
  512.8 4.4 copy-start.2
  517.2 10.2 copy-start.5
  521.8 5.6 copy-start.28
  536.8 98.9 %all-to-all-start.2 = ((f32[16,256,256]{2,0,1:T(8,128)}), f32[16,256,256]{2,0,1:T(8,128)}, u32[]{:S(2)}, u32[]{:S(2)}) async-start(f32[16,256,256]{2,0,1:T(8,128)} %copy.152), calls=%async_computation.2 | async-start | bytes 8388608 | tf_op jit(solution)/shard_map/all_to_all | solution.py:63
  541.6 7.5 copy-start.6
  635.6 98.8 %all-to-all-start.3 = ((f32[16,256,256]{2,0,1:T(8,128)}), f32[16,256,256]{2,0,1:T(8,128)}, u32[]{:S(2)}, u32[]{:S(2)}) async-start(f32[16,256,256]{2,0,1:T(8,128)} %copy.156), calls=%async_computation.3 | async-start | bytes 8388608 | tf_op jit(solution)/shard_map/all_to_all | solution.py:64
  640.4 6.0 copy-start.14
  734.4 99.0 %all-to-all-start.7 = ((f32[128,32,256]{2,1,0:T(8,128)}), f32[128,32,256]{2,1,0:T(8,128)}, u32[]{:S(2)}, u32[]{:S(2)}) async-start(f32[128,32,256]{2,1,0:T(8,128)} %copy.173), calls=%async_computation.7 | async-start | bytes 8388608 | tf_op jit(solution)/shard_map/all_to_all | solution.py:68
  742.2 8.4 copy-start.19
  746.6 4.0 copy-start.20
  833.4 98.7 %all-to-all-start.8 = ((f32[128,32,256]{2,1,0:T(8,128)}), f32[128,32,256]{2,1,0:T(8,128)}, u32[]{:S(2)}, u32[]{:S(2)}) async-start(f32[128,32,256]{2,1,0:T(8,128)} %copy.174), calls=%async_computation.8 | async-start | bytes 8388608 | tf_op jit(solution)/shard_map/all_to_all | solution.py:69
  838.1 6.0 copy-start.21
  1047.4 98.6 %all-to-all-start.11 = ((f32[16,256,256]{2,0,1:T(8,128)}), f32[16,256,256]{2,0,1:T(8,128)}, u32[]{:S(2)}, u32[]{:S(2)}) async-start(f32[16,256,256]{2,0,1:T(8,128)} %copy.181), calls=%async_computation.11 | async-start | bytes 8388608 | tf_op jit(solution)/shard_map/all_to_all | solution.py:76
  1146.0 99.0 %all-to-all-start.10 = ((f32[16,256,256]{2,0,1:T(8,128)}), f32[16,256,256]{2,0,1:T(8,128)}, u32[]{:S(2)}, u32[]{:S(2)}) async-start(f32[16,256,256]{2,0,1:T(8,128)} %copy.177), calls=%async_computation.10 | async-start | bytes 8388608 | tf_op jit(solution)/shard_map/all_to_all | solution.py:75
  1245.0 3.4 copy-start.15
  1248.0 4.5 copy-start.25
  1261.3 98.8 %all-to-all-start.13 = ((f32[128,32,256]{2,1,0:T(8,128)}), f32[128,32,256]{2,1,0:T(8,128)}, u32[]{:S(2)}, u32[]{:S(2)}) async-start(f32[128,32,256]{2,1,0:T(8,128)} %copy.187), calls=%async_computation.13 | async-start | bytes 8388608 | tf_op jit(solution)/shard_map/all_to_all | solution.py:81
  1266.0 6.0 copy-start.16
  1360.1 98.6 %all-to-all-start.12 = ((f32[128,32,256]{2,1,0:T(8,128)}), f32[128,32,256]{2,1,0:T(8,128)}, u32[]{:S(2)}, u32[]{:S(2)}) async-start(f32[128,32,256]{2,1,0:T(8,128)} %copy.184), calls=%async_computation.12 | async-start | bytes 8388608 | tf_op jit(solution)/shard_map/all_to_all | solution.py:80
  1465.9 5.1 copy-start.32
  1471.0 4.9 copy-start.11
  1471.0 4.9 copy-start.30
  1485.3 9.6 copy-start.7
  1490.1 4.8 copy-start.29
  1504.3 98.6 %all-to-all-start.14 = ((f32[16,256,256]{2,0,1:T(8,128)}), f32[16,256,256]{2,0,1:T(8,128)}, u32[]{:S(2)}, u32[]{:S(2)}) async-start(f32[16,256,256]{2,0,1:T(8,128)} %copy.194), calls=%async_computation.14 | async-start | bytes 8388608 | tf_op jit(solution)/shard_map/all_to_all | solution.py:63
  1508.9 7.5 copy-start.8
  1602.9 98.8 %all-to-all-start.15 = ((f32[16,256,256]{2,0,1:T(8,128)}), f32[16,256,256]{2,0,1:T(8,128)}, u32[]{:S(2)}, u32[]{:S(2)}) async-start(f32[16,256,256]{2,0,1:T(8,128)} %copy.198), calls=%async_computation.15 | async-start | bytes 8388608 | tf_op jit(solution)/shard_map/all_to_all | solution.py:64
  1704.5 4.0 copy-start.23
  1704.5 4.0 copy-start.22
  1717.1 99.0 %all-to-all-start.17 = ((f32[128,32,256]{2,1,0:T(8,128)}), f32[128,32,256]{2,1,0:T(8,128)}, u32[]{:S(2)}, u32[]{:S(2)}) async-start(f32[128,32,256]{2,1,0:T(8,128)} %copy.201), calls=%async_computation.17 | async-start | bytes 8388608 | tf_op jit(solution)/shard_map/all_to_all | solution.py:69
  1722.1 6.0 copy-start.24
  1931.4 98.6 %all-to-all-start.19 = ((f32[16,256,256]{2,0,1:T(8,128)}), f32[16,256,256]{2,0,1:T(8,128)}, u32[]{:S(2)}, u32[]{:S(2)}) async-start(f32[16,256,256]{2,0,1:T(8,128)} %copy.207), calls=%async_computation.19 | async-start | bytes 8388608 | tf_op jit(solution)/shard_map/all_to_all | solution.py:76
  2030.0 98.8 %all-to-all-start.18 = ((f32[16,256,256]{2,0,1:T(8,128)}), f32[16,256,256]{2,0,1:T(8,128)}, u32[]{:S(2)}, u32[]{:S(2)}) async-start(f32[16,256,256]{2,0,1:T(8,128)} %copy.203), calls=%async_computation.18 | async-start | bytes 8388608 | tf_op jit(solution)/shard_map/all_to_all | solution.py:75
  2128.8 3.4 copy-start.17
  2131.8 4.5 copy-start.26
  2144.9 99.0 %all-to-all-start.21 = ((f32[128,32,256]{2,1,0:T(8,128)}), f32[128,32,256]{2,1,0:T(8,128)}, u32[]{:S(2)}, u32[]{:S(2)}) async-start(f32[128,32,256]{2,1,0:T(8,128)} %copy.213), calls=%async_computation.21 | async-start | bytes 8388608 | tf_op jit(solution)/shard_map/all_to_all | solution.py:81
  2149.9 6.0 copy-start.18
  2243.9 98.6 %all-to-all-start.20 = ((f32[128,32,256]{2,1,0:T(8,128)}), f32[128,32,256]{2,1,0:T(8,128)}, u32[]{:S(2)}, u32[]{:S(2)}) async-start(f32[128,32,256]{2,1,0:T(8,128)} %copy.210), calls=%async_computation.20 | async-start | bytes 8388608 | tf_op jit(solution)/shard_map/all_to_all | solution.py:80
  2248.5 220.8 %all-reduce.4.cloned.1.call-start = ((), (), s32[]{:S(2)}) async-start(), calls=%async_computation.22 | async-start | bytes 8388608 | tf_op jit(solution)/shard_map/psum | solution.py:113
  2350.1 5.1 copy-start.33
  2355.2 4.9 copy-start.9
  2355.2 4.9 copy-start.31
  2469.4 7.6 copy-start.1
Sparse Core Ops, SparseCore 0:
  334.7 173.9 all-reduce.5
  2366.9 102.4 all-reduce.3
where the time goes:
time: 2490 us; the launch traced here: 2480 us
  waiting for transfers between devices  1670 us (67%)
  matrix products  297 us (12%)
  blocking collectives  196 us (8%)
  local copies, waits for them, and re-layouts  168 us (7%)
  starting transfers between devices  96 us (4%)
  other arithmetic  38.3 us (2%)
    dot_general x50, matrix products, along_axis(): jnp.einsum(einsum_forms[axis_index], values_in, table, precision=highest)  277 us
    all_to_all x3, waiting for transfers between devices, forward_transform(): lax.all_to_all(imag_part, 'brick', split_axis=1, concat_axis=0, tiled=True)  250 us
    all_to_all x3, waiting for transfers between devices, forward_transform(): lax.all_to_all(real_part, 'brick', split_axis=1, concat_axis=0, tiled=True)  229 us
    all_to_all x2, blocking collectives, forward_transform(): lax.all_to_all(depth_real, 'brick', split_axis=0, concat_axis=1, tiled=True)  196 us
    all_to_all x2, waiting for transfers between devices, inverse_transform(): lax.all_to_all(real_part, 'brick', split_axis=1, concat_axis=0, tiled=True)  178 us
    all_to_all x2, waiting for transfers between devices, inverse_transform(): lax.all_to_all(imag_part, 'brick', split_axis=1, concat_axis=0, tiled=True)  174 us
    all_to_all x3, waiting for transfers between devices, forward_transform(): lax.all_to_all(depth_imag, 'brick', split_axis=0, concat_axis=1, tiled=True)  159 us
    all_to_all x2, waiting for transfers between devices, inverse_transform(): lax.all_to_all(imag_part, 'brick', split_axis=0, concat_axis=1, tiled=True)  158 us
  transfers between devices with their start and end apart: 22, of which 21 were waited for; matrix products, arithmetic and copies ran while one was open for 13% of the time, Pallas kernels for 0%

commit v1 on v0

v1 whole, which is shorter than its diff:
```python
import math

import jax
import jax.numpy as jnp
from jax import lax
from jax.sharding import PartitionSpec as P

exact = lax.Precision.HIGH


def dft_tables(rows, columns, length):
    product = rows[:, None] * columns[None, :] % length
    angles = product.astype(jnp.float32) * (2.0 * math.pi / length)
    return jnp.cos(angles), jnp.sin(angles)


def exchange(values):
    return lax.all_to_all(values, "brick", split_axis=0, concat_axis=0)


def dot(form, left, right):
    return jnp.einsum(form, left, right, precision=exact)


def build(mesh):
    blocks, views = mesh.shape["brick"], mesh.shape["view"]

    def per_device(stack, spread, map_depth, map_rows, map_cols, start, stop):
        stack, spread = stack[0], spread[0]
        map_depth, map_rows, map_cols = map_depth[0], map_rows[0], map_cols[0]
        zb, ny, nx = stack.shape
        nz = zb * blocks
        yb = ny // blocks
        yq = yb // views
        half = nx // 2 + 1
        kb = -(-half // blocks)
        kx = kb * blocks

        index = lambda n: jnp.arange(n, dtype=jnp.int32)
        cx, sx = dft_tables(index(kx), index(nx), nx)
        valid = (index(kx) < half)[:, None].astype(jnp.float32)
        into_x = jnp.stack([cx * valid, -sx * valid])
        twice = jnp.where((index(kx) == 0) | (index(kx) == nx // 2), 1.0, 2.0)[:, None] * valid / nx
        from_x = jnp.stack([cx * twice, -sx * twice])
        cz, sz = dft_tables(index(nz), index(nz), nz)
        into_z = jnp.stack([jnp.stack([cz, -sz], 1), jnp.stack([sz, cz], 1)])
        from_z = jnp.stack([jnp.stack([cz, sz], 1), jnp.stack([-sz, cz], 1)]) / nz
        cy, sy = dft_tables(index(ny), index(ny), ny)
        into_z = into_z.reshape(2 * nz, 2 * nz)
        from_z = from_z.reshape(2 * nz, 2 * nz)

        def forward_pencil(values):
            rows = values.shape[0]
            real = dot("kx,yxz->ykz", into_x[0], values)
            imag = dot("kx,yxz->ykz", into_x[1], values)
            both = jnp.concatenate([real, imag], -1)
            both = dot("ykz,zw->kyw", both, into_z)
            return both.reshape(blocks, kb, rows, 2 * nz)

        def backward_pencil(values):
            both = dot("kyz,zw->ykw", values.reshape(kx, yb, 2 * nz), from_z)
            return dot("kx,ykz->yxz", from_x[0], both[..., :nz]) + dot(
                "kx,ykz->yxz", from_x[1], both[..., nz:]
            )

        def forward_rows(values):
            by_cos = dot("wy,kyz->kwz", cy, values)
            by_sin = dot("wy,kyz->kwz", sy, values)
            real = by_cos[..., :nz] + by_sin[..., nz:]
            imag = by_cos[..., nz:] - by_sin[..., :nz]
            return real, imag

        def backward_rows(real, imag):
            values = jnp.concatenate([real, imag], -1)
            by_cos = dot("wy,kyz->kwz", cy / ny, values)
            by_sin = dot("wy,kyz->kwz", sy / ny, values)
            real = by_cos[..., :nz] - by_sin[..., nz:]
            imag = by_cos[..., nz:] + by_sin[..., :nz]
            both = jnp.concatenate([real, imag], -1)
            return both.reshape(kb, blocks, yb, 2 * nz).transpose(1, 0, 2, 3)

        def gather_rows(values):
            return values.transpose(1, 0, 2, 3).reshape(kb, ny, 2 * nz)

        part = dot("zyx,ax->zya", stack, map_cols)
        part = dot("zyx,by->bzx", part, map_rows).reshape(blocks, yb, zb, nx)
        part = exchange(part)
        part = part.transpose(1, 0, 2, 3).reshape(yb, nz, nx)
        resampled = dot("yzx,cz->yxc", part, map_depth)

        first = lax.axis_index("brick") * yb
        depth = index(nz)
        from_depth = lax.dynamic_slice_in_dim(start[0], first, yb, 0)[:, :, None]
        to_depth = lax.dynamic_slice_in_dim(stop[0], first, yb, 0)[:, :, None]
        covered = ((depth >= from_depth) & (depth < to_depth)).astype(jnp.float32)
        view_weight = 0.05 + covered * (1.0 + jnp.log(1.0 + resampled * resampled))
        scatter = lambda values: lax.psum_scatter(
            values, "view", scatter_dimension=0, tiled=True
        )
        signal_part = scatter(view_weight * resampled)
        weight_part = scatter(view_weight)

        real = dot("zyx,kx->kyz", spread, into_x[0])
        imag = dot("zyx,kx->kyz", spread, into_x[1])
        real, imag = (
            dot("wy,kyz->kwz", cy, real) + dot("wy,kyz->kwz", sy, imag),
            dot("wy,kyz->kwz", cy, imag) - dot("wy,kyz->kwz", sy, real),
        )
        both = jnp.stack([real, imag]).reshape(2, blocks, kb, ny, zb)
        both = exchange(both.transpose(1, 2, 0, 4, 3))
        both = both.transpose(1, 2, 0, 3, 4).reshape(kb, 2 * nz, ny)
        otf = dot("kzy,zw->kyw", both, into_z)
        otf_real, otf_imag = otf[..., :nz], otf[..., nz:]

        joined = signal_part / weight_part
        spectrum = exchange(forward_pencil(joined))
        spectrum = lax.all_gather(spectrum, "view", axis=0)
        spectrum = spectrum.transpose(2, 1, 0, 3, 4).reshape(kb, ny, 2 * nz)
        real, imag = forward_rows(spectrum)
        blurred = backward_pencil(
            exchange(
                backward_rows(
                    real * otf_real - imag * otf_imag, real * otf_imag + imag * otf_real
                )
            )
        )
        ratio = resampled / blurred
        real, imag = forward_rows(gather_rows(exchange(forward_pencil(ratio))))
        correction = backward_pencil(
            exchange(
                backward_rows(
                    real * otf_real + imag * otf_imag, imag * otf_real - real * otf_imag
                )
            )
        )
        total = scatter(view_weight * correction)
        deconvolved = joined * total / weight_part

        def to_planes(values):
            values = values.transpose(2, 0, 1).reshape(blocks, zb, yq, nx)
            values = exchange(values)
            values = lax.all_gather(values, "view", axis=0)
            return values.transpose(2, 1, 0, 3, 4).reshape(zb, ny, nx)

        return to_planes(joined), to_planes(deconvolved)

    return per_device


def solution(mesh):
    whole, flat, plane = (
        P("view", "brick", None, None),
        P("view", None, None),
        P("brick", None, None),
    )
    return jax.shard_map(
        build(mesh),
        mesh=mesh,
        in_specs=(whole, whole, flat, flat, flat, flat, flat),
        out_specs=(plane, plane),
        check_vma=False,
    )
```

time: 2490 us -> 971 us (0.39)
  waiting for transfers between devices: 1670 us -> 493 us
  matrix products: 297 us -> 99 us
  local copies, waits for them, and re-layouts: 168 us -> 48.9 us
  starting transfers between devices: 96 us -> 21.5 us
  blocking collectives: 196 us -> 265 us
    all_to_all x20 -> x4, waiting for transfers between devices: 1500 us -> 303 us  [exchange(): return lax.all_to_all(values, 'brick', split_axis=0, concat_axis=0)]
    dot_general x53 -> x30, matrix products: 297 us -> 99 us  [dot(): return jnp.einsum(form, left, right, precision=exact)]
    psum x2 -> x0, waiting for transfers between devices: 171 us -> none  [the longest x1 103 us: per_device(): correction_total = lax.psum(view_weight * correction, 'view')]
    reduce_scatter x0 -> x3, waiting for transfers between devices: none -> 118 us  [per_device(): lax.psum_scatter(values, 'view', scatter_dimension=0, tiled=True)]
    all_to_all x20 -> x4, starting transfers between devices: 95.9 us -> 20.6 us  [exchange(): return lax.all_to_all(values, 'brick', split_axis=0, concat_axis=0)]
    all_gather x0 -> x3, waiting for transfers between devices: none -> 71.3 us  [the longest x2 71.3 us: to_planes(): values = lax.all_gather(values, 'view', axis=0)]
    all_to_all x2 -> x4, blocking collectives: 196 us -> 265 us  [exchange(): return lax.all_to_all(values, 'brick', split_axis=0, concat_axis=0)]
    all_to_all x16 -> x1, local copies, waits for them, and re-layouts: 55.4 us -> 2.82 us  [exchange(): return lax.all_to_all(values, 'brick', split_axis=0, concat_axis=0)]
  transfers between devices with their start and end apart: 22 -> 10, of which waited for: 21 -> 9; matrix products, arithmetic and copies ran while one was open for 13% -> 4% of each run, Pallas kernels for 0% -> 0%
where the time goes in v1:
time: 971 us; the launch traced here: 964 us
  waiting for transfers between devices  493 us (51%)
  blocking collectives  265 us (27%)
  matrix products  99 us (10%)
  local copies, waits for them, and re-layouts  48.9 us (5%)
  starting transfers between devices  21.5 us (2%)
  other arithmetic  20.9 us (2%)
  between operations  15.1 us (2%)
    all_to_all x4, waiting for transfers between devices, exchange(): return lax.all_to_all(values, 'brick', split_axis=0, concat_axis=0)  303 us
    all_to_all x4, blocking collectives, exchange(): return lax.all_to_all(values, 'brick', split_axis=0, concat_axis=0)  265 us
    reduce_scatter x3, waiting for transfers between devices, per_device(): lax.psum_scatter(values, 'view', scatter_dimension=0, tiled=True)  118 us
    dot_general x30, matrix products, dot(): return jnp.einsum(form, left, right, precision=exact)  99 us
    all_gather x2, waiting for transfers between devices, to_planes(): values = lax.all_gather(values, 'view', axis=0)  71.3 us
    all_to_all x4, starting transfers between devices, exchange(): return lax.all_to_all(values, 'brick', split_axis=0, concat_axis=0)  20.6 us
  transfers between devices with their start and end apart: 10, of which 9 were waited for; matrix products, arithmetic and copies ran while one was open for 4% of the time, Pallas kernels for 0%

profile of v1, /device:TPU:0, one launch (start us, length us, event | category | flops | bytes accessed | tf_op | source)
XLA Modules:
  0.0 963.6 jit_solution(17556025196105117504)
XLA Ops:
  8.1 4.0 fusion.12
  12.2 2.0 fusion.84
  14.2 4.4 copy.88
  18.6 6.3 all-to-all-start
  25.8 93.3 %all-to-all-done = f32[8,32,16,256]{3,2,1,0:T(8,128)} async-done(((f32[8,32,16,256]{3,2,1,0:T(8,128)}), f32[8,32,16,256]{3,2,1,0:T(8,128)}, u32[]{:S(2)}, u32[]{:S(2)}) %all-to-all-start) | async-done | bytes 4194336 | tf_op jit(solution)/shard_map/all_to_all | solution.py:18
  119.1 2.8 copy.89
  121.9 8.4 select_add_fusion
  131.1 2.0 fusion.170
  133.1 2.1 fusion.168
  136.6 4.9 fusion.61
  141.5 40.6 %reduce-scatter.6.cloned.1.call-done = f32[8,256,128]{2,1,0:T(8,128)} async-done(((f32[32,256,128]{2,1,0:T(8,128)}), f32[8,256,128]{2,1,0:T(8,128)}) %reduce-scatter.6.cloned.1.call-update) | async-done | bytes 1048592 | tf_op jit(solution)/shard_map/reduce_scatter | solution.py:97
  182.1 56.5 %reduce-scatter.4.cloned.1.call-done = f32[8,256,128]{2,1,0:T(8,128)} async-done(((f32[32,256,128]{2,1,0:T(8,128)}), f32[8,256,128]{2,1,0:T(8,128)}) %reduce-scatter.4.cloned.1.call-update) | async-done | bytes 1048592 | tf_op jit(solution)/shard_map/reduce_scatter | solution.py:97
  238.7 1.7 div.41
  244.2 5.0 all-to-all-start.2
  249.2 2.5 fusion.44
  251.8 2.5 fusion.42
  254.3 2.8 fusion.58
  257.1 2.5 fusion.52
  259.6 2.7 fusion.55
  262.4 2.7 maximum_bitcast_fusion
  265.1 11.9 %all-to-all-done.2 = f32[8,17,8,256]{3,2,1,0:T(8,128)} async-done(((f32[8,17,8,256]{3,2,1,0:T(8,128)}), f32[8,17,8,256]{3,2,1,0:T(8,128)}, u32[]{:S(2)}, u32[]{:S(2)}) %all-to-all-start.2) | async-done | bytes 1114144 | tf_op jit(solution)/shard_map/all_to_all | solution.py:18
  277.0 4.6 all-to-all-start.3
  282.3 98.9 %all-to-all-done.3 = f32[8,17,2,16,256]{4,3,1,2,0:T(8,128)} async-done(((f32[8,17,2,16,256]{4,3,1,2,0:T(8,128)}), f32[8,17,2,16,256]{4,3,1,2,0:T(8,128)}, u32[]{:S(2)}, u32[]{:S(2)}) %all-to-all-start.3) | async-done | bytes 4456480 | tf_op jit(solution)/shard_map/all_to_all | solution.py:18
  381.2 3.0 copy.103
  384.2 4.2 fusion.70
  388.4 2.9 copy.94
  391.3 4.5 convolution_bitcast_fusion.2
  395.9 4.5 convolution_bitcast_fusion.3
  400.4 1.9 multiply_subtract_fusion.1
  402.3 3.0 fusion.33
  405.3 3.0 fusion.34
  409.1 2.4 pad_maximum_fusion.1
  411.5 5.8 copy.105
  417.3 5.0 copy.106
  422.3 4.7 all-to-all-start.4
  427.9 98.7 %all-to-all-done.4 = f32[8,17,32,256]{3,2,1,0:T(8,128)} async-done(((f32[8,17,32,256]{3,2,1,0:T(8,128)}), f32[8,17,32,256]{3,2,1,0:T(8,128)}, u32[]{:S(2)}, u32[]{:S(2)}) %all-to-all-start.4) | async-done | bytes 4456480 | tf_op jit(solution)/shard_map/all_to_all | solution.py:18
  526.6 6.4 fusion.27
  533.0 2.4 fusion.23
  535.4 2.7 bitcast_divide_fusion
  538.1 1.7 convolution_bitcast_fusion.5
  539.8 1.9 convolution_bitcast_fusion.4
  541.8 2.0 fusion.37
  543.8 1.4 copy.110
  545.2 102.2 %all_to_all.40 = f32[8,17,32,256]{3,2,1,0:T(8,128)S(1)} all-to-all(f32[8,17,32,256]{3,2,1,0:T(8,128)S(1)} %bitcast.214), channel_id=1, replica_groups=mesh['view'=4,'brick'=8] {'brick'}, dimensions={0} | all-to-all | bytes 8912896 | tf_op jit(solution)/shard_map/all_to_all | solution.py:18
  648.0 4.5 convolution_bitcast_fusion
  652.6 4.5 convolution_bitcast_fusion.1
  657.1 1.6 multiply_add_fusion
  658.8 3.2 fusion.35
  662.0 3.0 fusion.36
  665.8 2.4 pad_maximum_fusion.3
  668.2 5.8 copy.114
  674.0 2.9 copy.115
  676.9 102.2 %all_to_all.41 = f32[8,17,32,256]{3,2,1,0:T(8,128)S(1)} all-to-all(f32[8,17,32,256]{3,2,1,0:T(8,128)S(1)} %copy.115), channel_id=1, replica_groups=mesh['view'=4,'brick'=8] {'brick'}, dimensions={0} | all-to-all | bytes 8912896 | tf_op jit(solution)/shard_map/all_to_all | solution.py:18
  779.1 4.3 fusion.30
  783.4 2.4 fusion.19
  785.9 5.7 bitcast_multiply_fusion
  792.1 29.7 %all_to_all.42 = f32[8,16,8,256]{3,2,1,0:T(8,128)} all-to-all(f32[8,16,8,256]{3,2,1,0:T(8,128)S(1)} %bitcast.228), channel_id=1, replica_groups=mesh['view'=4,'brick'=8] {'brick'}, dimensions={0} | all-to-all | bytes 2097152 | tf_op jit(solution)/shard_map/all_to_all | solution.py:18
  821.9 20.4 %reduce-scatter.8.cloned.1.call-done = f32[8,256,128]{2,1,0:T(8,128)} async-done(((f32[32,256,128]{2,1,0:T(8,128)}), f32[8,256,128]{2,1,0:T(8,128)}) %reduce-scatter.8.cloned.1.call-update) | async-done | bytes 1048592 | tf_op jit(solution)/shard_map/reduce_scatter | solution.py:97
  842.3 1.4 divide_bitcast_fusion
  844.2 31.1 %all_to_all.43 = f32[8,16,8,256]{3,2,1,0:T(8,128)} all-to-all(f32[8,16,8,256]{3,2,1,0:T(8,128)S(1)} %bitcast.227), channel_id=1, replica_groups=mesh['view'=4,'brick'=8] {'brick'}, dimensions={0} | all-to-all | bytes 2097152 | tf_op jit(solution)/shard_map/all_to_all | solution.py:18
  875.3 21.6 %all-gather.7.cloned.1.call-done = f32[32,16,8,256]{3,2,1,0:T(8,128)} async-done(((f32[8,16,8,256]{3,2,1,0:T(8,128)}), f32[32,16,8,256]{3,2,1,0:T(8,128)}) %all-gather.7.cloned.1.call-update) | async-done | bytes 4194320 | tf_op jit(solution)/shard_map/all_gather | solution.py:142
  896.9 4.8 copy.92
  901.7 49.7 %all-gather.11.cloned.1.call-done = f32[32,16,8,256]{3,2,1,0:T(8,128)} async-done(((f32[8,16,8,256]{3,2,1,0:T(8,128)}), f32[32,16,8,256]{3,2,1,0:T(8,128)}) %all-gather.11.cloned.1.call-update) | async-done | bytes 4194320 | tf_op jit(solution)/shard_map/all_gather | solution.py:142
  951.5 4.9 copy.120
  (72 shorter events, 12.6 us)
Async XLA Ops:
  7.2 1.0 copy-start
  7.2 5.0 copy-start.14
  18.6 100.4 %all-to-all-start = ((f32[8,32,16,256]{3,2,1,0:T(8,128)}), f32[8,32,16,256]{3,2,1,0:T(8,128)}, u32[]{:S(2)}, u32[]{:S(2)}) async-start(f32[8,32,16,256]{3,2,1,0:T(8,128)} %copy.88), calls=%async_computation | async-start | bytes 8388608 | tf_op jit(solution)/shard_map/all_to_all | solution.py:18
  25.0 157.2 %reduce-scatter.6.cloned.1.call-start = ((), (), s32[]{:S(2)}) async-start(), calls=%async_computation.12 | async-start | bytes 5242880 | tf_op jit(solution)/shard_map/reduce_scatter | solution.py:97
  25.8 96.1 %copy-start.10 = (s32[32,256]{1,0:T(8,128)}, s32[32,256]{1,0:T(8,128)S(1)}, u32[]{:S(2)}) copy-start(s32[32,256]{1,0:T(8,128)S(1)} %get-tuple-element.19) | copy-start | bytes 98308
  25.8 96.1 %copy-start.12 = (s32[32,256]{1,0:T(8,128)}, s32[32,256]{1,0:T(8,128)S(1)}, u32[]{:S(2)}) copy-start(s32[32,256]{1,0:T(8,128)S(1)} %get-tuple-element.20) | copy-start | bytes 98308
  25.8 96.1 %copy-start.15 = (f32[1,128,128]{2,1,0:T(8,128)S(1)}, f32[1,128,128]{2,1,0:T(8,128)}, u32[]{:S(2)}) copy-start(f32[1,128,128]{2,1,0:T(8,128)} %param.9) | copy-start | bytes 196612
  130.4 108.3 %reduce-scatter.4.cloned.1.call-start = ((), (), s32[]{:S(2)}) async-start(), calls=%async_computation.11 | async-start | bytes 5242880 | tf_op jit(solution)/shard_map/reduce_scatter | solution.py:97
  136.4 45.8 %copy-start.6 = (f32[2,128,2,128]{3,2,1,0:T(2,128)}, f32[2,128,2,128]{3,2,1,0:T(2,128)S(1)}, u32[]{:S(2)}) copy-start(f32[2,128,2,128]{3,2,1,0:T(2,128)S(1)} %pad_maximum_fusion.16) | copy-start | bytes 786436
  244.2 32.7 %all-to-all-start.2 = ((f32[8,17,8,256]{3,2,1,0:T(8,128)}), f32[8,17,8,256]{3,2,1,0:T(8,128)}, u32[]{:S(2)}, u32[]{:S(2)}) async-start(f32[8,17,8,256]{3,2,1,0:T(8,128)} %bitcast.222), calls=%async_computation.4 | async-start | bytes 2228224 | tf_op jit(solution)/shard_map/all_to_all | solution.py:18
  249.2 5.0 copy-start.2
  277.0 104.2 %all-to-all-start.3 = ((f32[8,17,2,16,256]{4,3,1,2,0:T(8,128)}), f32[8,17,2,16,256]{4,3,1,2,0:T(8,128)}, u32[]{:S(2)}, u32[]{:S(2)}) async-start(f32[8,17,2,16,256]{4,3,1,2,0:T(8,128)} %maximum_bitcast_fusion), calls=%async_computation.5 | async-start | bytes 8912896 | tf_op jit(solution)/shard_map/all_to_all | solution.py:18
  281.5 106.8 %all-gather.9.cloned.1.call-start = ((), (), s32[]{:S(2)}) async-start(), calls=%async_computation.15 | async-start | bytes 5570560 | tf_op jit(solution)/shard_map/all_gather | solution.py:117
  381.2 3.0 copy-start.7
  391.3 9.1 slice-start
  395.9 4.5 slice-start.1
  422.3 5.2 copy-start.8
  422.3 5.2 copy-start.9
  422.3 104.3 %all-to-all-start.4 = ((f32[8,17,32,256]{3,2,1,0:T(8,128)}), f32[8,17,32,256]{3,2,1,0:T(8,128)}, u32[]{:S(2)}, u32[]{:S(2)}) async-start(f32[8,17,32,256]{3,2,1,0:T(8,128)} %copy.106), calls=%async_computation.6 | async-start | bytes 8912896 | tf_op jit(solution)/shard_map/all_to_all | solution.py:18
  427.0 415.3 %reduce-scatter.8.cloned.1.call-start = ((), (), s32[]{:S(2)}) async-start(), calls=%async_computation.13 | async-start | bytes 5242880 | tf_op jit(solution)/shard_map/reduce_scatter | solution.py:97
  533.0 2.4 copy-start.3
  648.0 9.1 slice-start.2
  652.6 4.5 slice-start.3
  783.4 2.5 copy-start.4
  783.4 2.5 copy-start.11
  783.4 2.5 copy-start.13
  791.6 50.7 %copy-start.5 = (f32[8,256,128]{2,1,0:T(8,128)S(1)}, f32[8,256,128]{2,1,0:T(8,128)}, u32[]{:S(2)}) copy-start(f32[8,256,128]{2,1,0:T(8,128)} %reduce-scatter.6.cloned.1.call-done) | copy-start | bytes 3145732
  791.6 105.3 %all-gather.7.cloned.1.call-start = ((), (), s32[]{:S(2)}) async-start(), calls=%async_computation.14 | async-start | bytes 5242880 | tf_op jit(solution)/shard_map/all_gather | solution.py:142
  821.9 129.6 %all-gather.11.cloned.1.call-start = ((), (), s32[]{:S(2)}) async-start(), calls=%async_computation.16 | async-start | bytes 5242880 | tf_op jit(solution)/shard_map/all_gather | solution.py:142
  951.5 4.9 copy-start.1
Sparse Core Ops, SparseCore 0:
  130.5 51.6 reduce-scatter.5
  185.9 52.6 reduce-scatter.3
  284.2 55.2 all-gather.8
  791.7 50.5 reduce-scatter.7
  844.2 52.6 all-gather.6
  898.7 52.6 all-gather.10

commit v2 on v1

--- a/solution.py
+++ b/solution.py
@@ -1,8 +1,11 @@
+import functools
 import math
 
 import jax
 import jax.numpy as jnp
 from jax import lax
+from jax.experimental import pallas as pl
+from jax.experimental.pallas import tpu as pltpu
 from jax.sharding import PartitionSpec as P
 
 exact = lax.Precision.HIGH
@@ -20,6 +23,98 @@
 
 def dot(form, left, right):
     return jnp.einsum(form, left, right, precision=exact)
+
+
+def halves(values):
+    top = values.astype(jnp.bfloat16)
+    return top, (values - top.astype(jnp.float32)).astype(jnp.bfloat16)
+
+
+def pair_dot(left, right):
+    once = lambda a, b: jnp.dot(a, b, preferred_element_type=jnp.float32)
+    return once(left[0], right[0]) + (once(left[0], right[1]) + once(left[1], right[0]))
+
+
+def rows_kernel(sign, values, transfer, forth_hi, forth_lo, back_hi, back_lo, out):
+    ny, nz = transfer.shape[1], transfer.shape[2] // 2
+    spectrum = pair_dot((forth_hi[...], forth_lo[...]), halves(values[...].reshape(ny, 2 * nz)))
+    real = spectrum[:ny, :nz] + spectrum[ny:, nz:]
+    imag = spectrum[:ny, nz:] - spectrum[ny:, :nz]
+    otf_real, otf_imag = transfer[0, :, :nz], sign * transfer[0, :, nz:]
+    product = jnp.concatenate(
+        [real * otf_real - imag * otf_imag, real * otf_imag + imag * otf_real], -1
+    )
+    spectrum = pair_dot((back_hi[...], back_lo[...]), halves(product))
+    real = spectrum[:ny, :nz] - spectrum[ny:, nz:]
+    imag = spectrum[:ny, nz:] + spectrum[ny:, :nz]
+    out[...] = jnp.concatenate([real, imag], -1).reshape(out.shape)
+
+
+def pencil_back(values, z_table, x_table):
+    kx, rows, nz = values.shape[0], values.shape[1], values.shape[2] // 2
+    flat = pair_dot(halves(values[...].reshape(kx * rows, 2 * nz)), z_table)
+    turned = jnp.swapaxes(flat.reshape(kx, rows, 2 * nz), 0, 1)
+    wide = jnp.concatenate(
+        [
+            jnp.concatenate([turned[row, :, part * nz : (part + 1) * nz] for row in range(rows)], -1)
+            for part in range(2)
+        ],
+        0,
+    )
+    return pair_dot(x_table, halves(wide))
+
+
+def pencil_forth(wide, x_table, z_table, out):
+    kx, rows, nz = out.shape[0], out.shape[1], out.shape[2] // 2
+    lines = pair_dot(x_table, halves(wide))
+    turned = jnp.stack(
+        [
+            jnp.concatenate(
+                [lines[part * kx : (part + 1) * kx, row * nz : (row + 1) * nz] for part in range(2)], -1
+            )
+            for row in range(rows)
+        ],
+        0,
+    )
+    flat = jnp.swapaxes(turned, 0, 1).reshape(kx * rows, 2 * nz)
+    out[...] = pair_dot(halves(flat), z_table).reshape(kx, rows, 2 * nz)
+
+
+def widen(values):
+    return jnp.concatenate([values[row] for row in range(values.shape[0])], -1)
+
+
+def ratio_kernel(values, resampled, bz, bzl, bx, bxl, fx, fxl, fz, fzl, out):
+    wide = pencil_back(values, (bz[...], bzl[...]), (bx[...], bxl[...]))
+    pencil_forth(
+        widen(resampled) / wide, (fx[...], fxl[...]), (fz[...], fzl[...]), out
+    )
+
+
+def weigh_kernel(values, weight, bz, bzl, bx, bxl, out):
+    rows, nz = weight.shape[0], weight.shape[2]
+    wide = pencil_back(values, (bz[...], bzl[...]), (bx[...], bxl[...]))
+    for row in range(rows):
+        out[row] = weight[row] * wide[:, row * nz : (row + 1) * nz]
+
+
+def forth_kernel(values, fx, fxl, fz, fzl, out):
+    pencil_forth(widen(values), (fx[...], fxl[...]), (fz[...], fzl[...]), out)
+
+
+def call(kernel, grid, specs, out_shape, out_spec, operands):
+    return pl.pallas_call(
+        kernel,
+        grid=(grid,),
+        in_specs=specs,
+        out_specs=out_spec,
+        out_shape=jax.ShapeDtypeStruct(out_shape, jnp.float32),
+        compiler_params=pltpu.CompilerParams(vmem_limit_bytes=48 << 20),
+    )(*operands)
+
+
+def fixed(table):
+    return pl.BlockSpec(table.shape, lambda step: (0,) * table.ndim)
 
 
 def build(mesh):
@@ -82,12 +177,94 @@
         def gather_rows(values):
             return values.transpose(1, 0, 2, 3).reshape(kb, ny, 2 * nz)
 
+        tiled = yb % 8 == 0 and yq % 8 == 0 and kx % 8 == 0 and nz % 128 == 0
+        rows = 8
+        z_forth, z_back = halves(into_z), halves(from_z)
+        x_forth = halves(into_x.reshape(2 * kx, nx))
+        x_back = halves(from_x.reshape(2 * kx, nx).T)
+        both_y = jnp.concatenate([cy, sy], 0)
+        y_forth, y_back = halves(both_y), halves(both_y / ny)
+        y_mixed = tuple(
+            table.reshape(2 * ny, blocks, views, yq).swapaxes(1, 2).reshape(2 * ny, ny)
+            for table in y_forth
+        )
+        lines_spec = pl.BlockSpec((kx, rows, 2 * nz), lambda step: (0, step, 0))
+        cells_spec = pl.BlockSpec((rows, nx, nz), lambda step: (step, 0, 0))
+
+        def forth_lines(values):
+            if not tiled:
+                return forward_pencil(values)
+            tables = x_forth + z_forth
+            count = values.shape[0]
+            lines = call(
+                forth_kernel, count // rows, [cells_spec] + [fixed(t) for t in tables],
+                (kx, count, 2 * nz), lines_spec, (values,) + tables,
+            )
+            return lines.reshape(blocks, kb, count, 2 * nz)
+
+        def ratio_lines(values):
+            if not tiled:
+                return forward_pencil(resampled / backward_pencil(values))
+            tables = z_back + x_back + x_forth + z_forth
+            lines = call(
+                ratio_kernel, yb // rows,
+                [lines_spec, cells_spec] + [fixed(t) for t in tables],
+                (kx, yb, 2 * nz), lines_spec,
+                (values.reshape(kx, yb, 2 * nz), resampled) + tables,
+            )
+            return lines.reshape(blocks, kb, yb, 2 * nz)
+
+        def weighed_lines(values):
+            if not tiled:
+                return view_weight * backward_pencil(values)
+            tables = z_back + x_back
+            return call(
+                weigh_kernel, yb // rows,
+                [lines_spec, cells_spec] + [fixed(t) for t in tables],
+                (yb, nx, nz), cells_spec,
+                (values.reshape(kx, yb, 2 * nz), view_weight) + tables,
+            )
+
+        def filter_rows(values, otf, sign, gathered):
+            if not tiled:
+                if gathered:
+                    values = values.transpose(2, 1, 0, 3, 4).reshape(kb, ny, 2 * nz)
+                else:
+                    values = gather_rows(values)
+                real, imag = forward_rows(values)
+                otf_real, otf_imag = otf[..., :nz], sign * otf[..., nz:]
+                return backward_rows(
+                    real * otf_real - imag * otf_imag, real * otf_imag + imag * otf_real
+                )
+            spec = pl.BlockSpec((blocks, 1, yb, 2 * nz), lambda step: (0, step, 0, 0))
+            taken, forth = spec, y_forth
+            if gathered:
+                taken = pl.BlockSpec(
+                    (views, blocks, 1, yq, 2 * nz), lambda step: (0, 0, step, 0, 0)
+                )
+                forth = y_mixed
+            tables = forth + y_back
+            return call(
+                functools.partial(rows_kernel, sign), kb,
+                [taken, pl.BlockSpec((1, ny, 2 * nz), lambda step: (step, 0, 0))]
+                + [fixed(t) for t in tables],
+                (blocks, kb, yb, 2 * nz), spec, (values, otf) + tables,
+            )
+
         part = dot("zyx,ax->zya", stack, map_cols)
         part = dot("zyx,by->bzx", part, map_rows).reshape(blocks, yb, zb, nx)
-        part = exchange(part)
+        real = dot("zyx,kx->kyz", spread, into_x[0])
+        imag = dot("zyx,kx->kyz", spread, into_x[1])
+        real, imag = (
+            dot("wy,kyz->kwz", cy, real) + dot("wy,kyz->kwz", sy, imag),
+            dot("wy,kyz->kwz", cy, imag) - dot("wy,kyz->kwz", sy, real),
+        )
+        both = jnp.stack([real, imag]).reshape(2, blocks, kb, ny, zb).transpose(1, 2, 0, 4, 3)
+        part, both = lax.optimization_barrier((exchange(part), both))
+        both = exchange(both)
+
         part = part.transpose(1, 0, 2, 3).reshape(yb, nz, nx)
         resampled = dot("yzx,cz->yxc", part, map_depth)
-
         first = lax.axis_index("brick") * yb
         depth = index(nz)
         from_depth = lax.dynamic_slice_in_dim(start[0], first, yb, 0)[:, :, None]
@@ -99,50 +276,34 @@
         )
         signal_part = scatter(view_weight * resampled)
         weight_part = scatter(view_weight)
-
-        real = dot("zyx,kx->kyz", spread, into_x[0])
-        imag = dot("zyx,kx->kyz", spread, into_x[1])
-        real, imag = (
-            dot("wy,kyz->kwz", cy, real) + dot("wy,kyz->kwz", sy, imag),
-            dot("wy,kyz->kwz", cy, imag) - dot("wy,kyz->kwz", sy, real),
-        )
-        both = jnp.stack([real, imag]).reshape(2, blocks, kb, ny, zb)
-        both = exchange(both.transpose(1, 2, 0, 4, 3))
+        signal_part, weight_part, both = lax.optimization_barrier((signal_part, weight_part, both))
+
         both = both.transpose(1, 2, 0, 3, 4).reshape(kb, 2 * nz, ny)
         otf = dot("kzy,zw->kyw", both, into_z)
-        otf_real, otf_imag = otf[..., :nz], otf[..., nz:]
-
-        joined = signal_part / weight_part
-        spectrum = exchange(forward_pencil(joined))
-        spectrum = lax.all_gather(spectrum, "view", axis=0)
-        spectrum = spectrum.transpose(2, 1, 0, 3, 4).reshape(kb, ny, 2 * nz)
-        real, imag = forward_rows(spectrum)
-        blurred = backward_pencil(
-            exchange(
-                backward_rows(
-                    real * otf_real - imag * otf_imag, real * otf_imag + imag * otf_real
-                )
-            )
-        )
-        ratio = resampled / blurred
-        real, imag = forward_rows(gather_rows(exchange(forward_pencil(ratio))))
-        correction = backward_pencil(
-            exchange(
-                backward_rows(
-                    real * otf_real + imag * otf_imag, imag * otf_real - real * otf_imag
-                )
-            )
-        )
-        total = scatter(view_weight * correction)
-        deconvolved = joined * total / weight_part
-
-        def to_planes(values):
-            values = values.transpose(2, 0, 1).reshape(blocks, zb, yq, nx)
-            values = exchange(values)
+
+        def by_planes(values):
+            return values.transpose(2, 0, 1).reshape(blocks, zb, yq, nx)
+
+        def whole_planes(values):
             values = lax.all_gather(values, "view", axis=0)
             return values.transpose(2, 1, 0, 3, 4).reshape(zb, ny, nx)
 
-        return to_planes(joined), to_planes(deconvolved)
+        joined = signal_part / weight_part
+        spectrum = exchange(forth_lines(joined))
+        spectrum, planes = lax.optimization_barrier((spectrum, by_planes(joined)))
+        planes = exchange(planes)
+        spectrum = lax.all_gather(spectrum, "view", axis=0)
+        products, planes = lax.optimization_barrier(
+            (filter_rows(spectrum, otf, 1.0, True), planes)
+        )
+        products, joined_out = lax.optimization_barrier(
+            (exchange(products), whole_planes(planes))
+        )
+        products = exchange(ratio_lines(products))
+        products = exchange(filter_rows(products, otf, -1.0, False))
+        total = scatter(weighed_lines(products))
+        deconvolved = joined * total / weight_part
+        return joined_out, whole_planes(exchange(by_planes(deconvolved)))
 
     return per_device
 

time: 971 us -> 870 us (0.90)
  blocking collectives: 265 us -> 134 us
  Pallas kernels: 0 us -> 72.6 us
  matrix products: 99 us -> 38.3 us
  waiting for transfers between devices: 493 us -> 522 us
  local copies, waits for them, and re-layouts: 48.9 us -> 34 us
    all_to_all x4 -> x2, blocking collectives: 265 us -> 134 us  [exchange(): return lax.all_to_all(values, 'brick', split_axis=0, concat_axis=0)]
    pallas_call x0 -> x5, Pallas kernels: none -> 72.6 us  [call(): pl.pallas_call(kernel, grid=(grid,), in_specs=specs, out_specs=out_spec,...]
    reduce_scatter x3, waiting for transfers between devices: 118 us -> 54 us  [per_device(): lax.psum_scatter(values, 'view', scatter_dimension=0, tiled=True)]
    dot_general x30 -> x10, matrix products: 99 us -> 38.3 us  [dot(): return jnp.einsum(form, left, right, precision=exact)]
    all_gather x1, waiting for transfers between devices: 0.01 us -> 36 us  [per_device(): spectrum = lax.all_gather(spectrum, 'view', axis=0)]
    all_gather x2, waiting for transfers between devices: 71.3 us -> 101 us  [whole_planes(): values = lax.all_gather(values, 'view', axis=0)]
    all_to_all x4 -> x6, waiting for transfers between devices: 303 us -> 329 us  [exchange(): return lax.all_to_all(values, 'brick', split_axis=0, concat_axis=0)]
    transpose x11 -> x4, local copies, waits for them, and re-layouts: 27.9 us -> 11.6 us  [the longest x2 9.73 us: whole_planes(): return values.transpose(2, 1, 0, 3, 4).reshape(zb, ny, nx)]
  transfers between devices with their start and end apart: 10 -> 12, of which waited for: 9 -> 10; matrix products, arithmetic and copies ran while one was open for 4% -> 6% of each run, Pallas kernels for 0% -> 2%
where the time goes in v2:
time: 870 us; the launch traced here: 864 us
  waiting for transfers between devices  522 us (60%)
  blocking collectives  134 us (15%)
  Pallas kernels  72.6 us (8%)
  matrix products  38.3 us (4%)
  local copies, waits for them, and re-layouts  34 us (4%)
  starting transfers between devices  30.1 us (3%)
  other arithmetic  18.2 us (2%)
  between operations  14.7 us (2%)
    all_to_all x6, waiting for transfers between devices, exchange(): return lax.all_to_all(values, 'brick', split_axis=0, concat_axis=0)  329 us
    all_to_all x2, blocking collectives, exchange(): return lax.all_to_all(values, 'brick', split_axis=0, concat_axis=0)  134 us
    all_gather x2, waiting for transfers between devices, whole_planes(): values = lax.all_gather(values, 'view', axis=0)  101 us
    pallas_call x5, Pallas kernels, call(): pl.pallas_call(kernel, grid=(grid,), in_specs=specs, out_specs=out_spec,...  72.6 us
    reduce_scatter x3, waiting for transfers between devices, per_device(): lax.psum_scatter(values, 'view', scatter_dimension=0, tiled=True)  54 us
    dot_general x10, matrix products, dot(): return jnp.einsum(form, left, right, precision=exact)  38.3 us
    all_gather x1, waiting for transfers between devices, per_device(): spectrum = lax.all_gather(spectrum, 'view', axis=0)  36 us
    all_to_all x6, starting transfers between devices, exchange(): return lax.all_to_all(values, 'brick', split_axis=0, concat_axis=0)  29.5 us
  transfers between devices with their start and end apart: 12, of which 10 were waited for; matrix products, arithmetic and copies ran while one was open for 6% of the time, Pallas kernels for 2%

profile of v2, /device:TPU:0, one launch (start us, length us, event | category | flops | bytes accessed | tf_op | source)
XLA Modules:
  0.0 864.0 jit_solution(12360289499693635485)
XLA Ops:
  7.2 0.9 copy-done
  8.1 4.0 fusion.4
  12.2 2.1 fusion.42
  14.2 4.4 copy.34
  18.7 6.3 all-to-all-start
  25.2 0.8 dynamic-slice_bitcast_fusion
  26.0 4.9 fusion.24
  30.9 2.5 fusion.7
  33.4 2.5 fusion.9
  36.0 2.8 fusion.21
  38.8 2.8 fusion.15
  41.5 2.6 fusion.18
  44.1 2.6 maximum_bitcast_fusion
  46.7 72.4 %all-to-all-done = f32[8,32,16,256]{3,2,1,0:T(8,128)} async-done(((f32[8,32,16,256]{3,2,1,0:T(8,128)}), f32[8,32,16,256]{3,2,1,0:T(8,128)}, u32[]{:S(2)}, u32[]{:S(2)}) %all-to-all-start) | async-done | bytes 4194336 | tf_op jit(solution)/shard_map/all_to_all | solution.py:21
  119.1 2.8 copy.41
  121.9 8.4 select_add_fusion
  130.4 0.7 reduce-scatter.6.cloned.1.call-update
  131.1 4.6 all-to-all-start.1
  135.7 2.0 fusion.97
  137.7 1.9 fusion.96
  139.6 2.0 fusion.95
  141.6 0.3 fusion.74
  141.9 1.0 pad_maximum_fusion.4
  142.9 0.6 broadcast_multiply_fusion.1
  143.6 91.7 %all-to-all-done.1 = f32[8,17,2,16,256]{4,3,2,1,0:T(8,128)} async-done(((f32[8,17,2,16,256]{4,3,2,1,0:T(8,128)}), f32[8,17,2,16,256]{4,3,2,1,0:T(8,128)}, u32[]{:S(2)}, u32[]{:S(2)}) %all-to-all-start.1) | async-done | bytes 4456480 | tf_op jit(solution)/shard_map/all_to_all | solution.py:21
  235.3 3.3 reduce-scatter.6.cloned.1.call-done
  238.6 1.7 div.28.values
  240.3 2.2 shard_map.86
  242.5 4.6 all-to-all-start.2
  247.2 1.4 copy.43
  248.6 26.6 %all-to-all-done.2 = f32[8,17,8,256]{3,2,1,0:T(8,128)S(1)} async-done(((f32[8,17,8,256]{3,2,1,0:T(8,128)}), f32[8,17,8,256]{3,2,1,0:T(8,128)S(1)}, u32[]{:S(2)}, u32[]{:S(2)}) %all-to-all-start.2) | async-done | bytes 1114144 | tf_op jit(solution)/shard_map/all_to_all | solution.py:21
  275.2 1.0 copy-done.6
  276.2 4.7 all-to-all-start.3
  280.8 0.9 reshape.387
  281.8 1.1 fusion.76
  283.2 1.0 fusion.77
  284.4 3.0 copy.44
  287.4 5.7 fusion.126.transfer
  293.1 36.0 %all-gather.7.cloned.1.call-done = f32[32,17,8,256]{3,2,1,0:T(8,128)} async-done(((f32[8,17,8,256]{3,2,1,0:T(8,128)}), f32[32,17,8,256]{3,2,1,0:T(8,128)}) %all-gather.7.cloned.1.call-update) | async-done | bytes 4456464 | tf_op jit(solution)/shard_map/all_gather | solution.py:295
  329.1 19.8 %shard_map.87 = f32[8,17,32,256]{3,2,1,0:T(8,128)S(1)} custom-call(f32[4,8,17,8,256]{4,3,2,1,0:T(8,128)} %bitcast.152, f32[17,256,256]{2,1,0:T(8,128)} %fusion.126.transfer, bf16[512,256]{1,0:T(8,128)(2,1)S(1)} %copy.46.forth_hi, bf16[512,256]{1,0:T(8,128)(2,1)S(1)} %copy.47.forth_lo, bf16[512,256]{1,0:T(8,128)(2,1)S(1)} %get-tuple-element.32.back_hi, ...), custom_call_target="tpu_custom_call" | custom-call | tf_op jit(solution)/shard_map/pallas_call | solution.py:106
  348.9 2.2 copy-done.2
  351.1 4.7 all-to-all-start.4
  355.9 0.5 all-gather.9.cloned.1.call-update
  356.4 0.6 broadcast_multiply_fusion
  357.0 0.7 pad_maximum_fusion.3
  357.7 1.9 copy.49
  359.7 1.0 fusion.28
  360.7 50.7 %all-gather.9.cloned.1.call-done = f32[32,16,8,256]{3,2,1,0:T(8,128)} async-done(((f32[8,16,8,256]{3,2,1,0:T(8,128)}), f32[32,16,8,256]{3,2,1,0:T(8,128)}) %all-gather.9.cloned.1.call-update) | async-done | bytes 4194320 | tf_op jit(solution)/shard_map/all_gather | solution.py:288
  411.4 4.8 copy.48
  416.3 39.3 %all-to-all-done.4 = f32[8,17,32,256]{3,2,1,0:T(8,128)} async-done(((f32[8,17,32,256]{3,2,1,0:T(8,128)}), f32[8,17,32,256]{3,2,1,0:T(8,128)}, u32[]{:S(2)}, u32[]{:S(2)}) %all-to-all-start.4) | async-done | bytes 4456480 | tf_op jit(solution)/shard_map/all_to_all | solution.py:21
  455.6 2.2 copy-done.4
  457.8 19.5 %shard_map.88 = f32[136,32,256]{2,1,0:T(8,128)} custom-call(f32[136,32,256]{2,1,0:T(8,128)} %bitcast.43.values, f32[32,256,128]{2,1,0:T(8,128)S(1)} %copy-done.4, bf16[256,256]{1,0:T(8,128)(2,1)S(1)} %bitcast.141, bf16[256,256]{1,0:T(8,128)(2,1)S(1)} %fusion.36.bzl, bf16[256,272]{1,0:T(8,128)(2,1)S(1)} %get-tuple-element.25.bx, ...), custom_call_target="tpu_custom_call" | custom-call | tf_op jit(solution)/shard_map/pallas_call | solution.py:106
  477.2 4.6 all-to-all-start.5
  482.1 99.4 %all-to-all-done.5.values = f32[8,17,32,256]{3,2,1,0:T(8,128)} async-done(((f32[8,17,32,256]{3,2,1,0:T(8,128)}), f32[8,17,32,256]{3,2,1,0:T(8,128)}, u32[]{:S(2)}, u32[]{:S(2)}) %all-to-all-start.5) | async-done | bytes 4456480 | tf_op jit(solution)/shard_map/all_to_all | solution.py:21
  581.5 19.9 %shard_map.89 = f32[8,17,32,256]{3,2,1,0:T(8,128)S(1)} custom-call(f32[8,17,32,256]{3,2,1,0:T(8,128)} %all-to-all-done.5.values, f32[17,256,256]{2,1,0:T(8,128)} %fusion.126.transfer, bf16[512,256]{1,0:T(8,128)(2,1)S(1)} %fusion.51.forth_hi, bf16[512,256]{1,0:T(8,128)(2,1)S(1)} %get-tuple-element.30.forth_lo, ...), custom_call_target="tpu_custom_call" | custom-call | tf_op jit(solution)/shard_map/pallas_call | solution.py:106
  601.3 103.0 %all_to_all.40 = f32[8,17,32,256]{3,2,1,0:T(8,128)} all-to-all(f32[8,17,32,256]{3,2,1,0:T(8,128)S(1)} %shard_map.89), channel_id=1, replica_groups=mesh['view'=4,'brick'=8] {'brick'}, dimensions={0} | all-to-all | bytes 8912896 | tf_op jit(solution)/shard_map/all_to_all | solution.py:21
  704.3 11.3 %shard_map.90 = f32[32,256,128]{2,1,0:T(8,128)S(1)} custom-call(f32[136,32,256]{2,1,0:T(8,128)} %bitcast.146, f32[32,256,128]{2,1,0:T(8,128)} %get-tuple-element.28.weight, bf16[256,256]{1,0:T(8,128)(2,1)S(1)} %bitcast.142, bf16[256,256]{1,0:T(8,128)(2,1)S(1)} %fusion.36.bzl, bf16[256,272]{1,0:T(8,128)(2,1)S(1)} %get-tuple-element.25.bx, ...), custom_call_target="tpu_custom_call" | custom-call | tf_op jit(solution)/shard_map/pallas_call | solution.py:106
  715.6 2.0 copy-done.3
  717.7 50.7 %reduce-scatter.8.cloned.1.call-done = f32[8,256,128]{2,1,0:T(8,128)} async-done(((f32[32,256,128]{2,1,0:T(8,128)}), f32[8,256,128]{2,1,0:T(8,128)}) %reduce-scatter.8.cloned.1.call-update) | async-done | bytes 1048592 | tf_op jit(solution)/shard_map/reduce_scatter | solution.py:274
  768.3 1.4 divide_bitcast_fusion
  769.7 0.5 copy.50
  770.2 31.1 %all_to_all.41 = f32[8,16,8,256]{3,2,1,0:T(8,128)} all-to-all(f32[8,16,8,256]{3,2,1,0:T(8,128)S(1)} %bitcast.158), channel_id=1, replica_groups=mesh['view'=4,'brick'=8] {'brick'}, dimensions={0} | all-to-all | bytes 2097152 | tf_op jit(solution)/shard_map/all_to_all | solution.py:21
  801.3 50.8 %all-gather.11.cloned.1.call-done = f32[32,16,8,256]{3,2,1,0:T(8,128)} async-done(((f32[8,16,8,256]{3,2,1,0:T(8,128)}), f32[32,16,8,256]{3,2,1,0:T(8,128)}) %all-gather.11.cloned.1.call-update) | async-done | bytes 4194320 | tf_op jit(solution)/shard_map/all_gather | solution.py:288
  852.1 4.9 copy.51
  (46 shorter events, 1.3 us)
Async XLA Ops:
  7.2 1.0 copy-start
  7.2 5.0 copy-start.10
  18.7 100.4 %all-to-all-start = ((f32[8,32,16,256]{3,2,1,0:T(8,128)}), f32[8,32,16,256]{3,2,1,0:T(8,128)}, u32[]{:S(2)}, u32[]{:S(2)}) async-start(f32[8,32,16,256]{3,2,1,0:T(8,128)} %copy.34), calls=%async_computation | async-start | bytes 8388608 | tf_op jit(solution)/shard_map/all_to_all | solution.py:21
  25.0 210.4 %reduce-scatter.4.cloned.1.call-start = ((), (), s32[]{:S(2)}) async-start(), calls=%async_computation.11 | async-start | bytes 5242880 | tf_op jit(solution)/shard_map/reduce_scatter | solution.py:274
  30.9 5.0 copy-start.5
  46.7 75.2 %copy-start.11 = (f32[1,128,128]{2,1,0:T(8,128)S(1)}, f32[1,128,128]{2,1,0:T(8,128)}, u32[]{:S(2)}) copy-start(f32[1,128,128]{2,1,0:T(8,128)} %param.9) | copy-start | bytes 196612
  130.3 108.3 %reduce-scatter.6.cloned.1.call-start = ((), (), s32[]{:S(2)}) async-start(), calls=%async_computation.12 | async-start | bytes 5242880 | tf_op jit(solution)/shard_map/reduce_scatter | solution.py:274
  131.1 104.2 %all-to-all-start.1 = ((f32[8,17,2,16,256]{4,3,2,1,0:T(8,128)}), f32[8,17,2,16,256]{4,3,2,1,0:T(8,128)}, u32[]{:S(2)}, u32[]{:S(2)}) async-start(f32[8,17,2,16,256]{4,3,2,1,0:T(8,128)} %maximum_bitcast_fusion), calls=%async_computation.3 | async-start | bytes 8912896 | tf_op jit(solution)/shard_map/all_to_all | solution.py:21
  242.5 32.6 %all-to-all-start.2 = ((f32[8,17,8,256]{3,2,1,0:T(8,128)}), f32[8,17,8,256]{3,2,1,0:T(8,128)S(1)}, u32[]{:S(2)}, u32[]{:S(2)}) async-start(f32[8,17,8,256]{3,2,1,0:T(8,128)} %bitcast.30), calls=%async_computation.4 | async-start | bytes 2228224 | tf_op jit(solution)/shard_map/all_to_all | solution.py:21
  247.2 82.0 %all-gather.7.cloned.1.call-start = ((), (), s32[]{:S(2)}) async-start(), calls=%async_computation.14 | async-start | bytes 5570560 | tf_op jit(solution)/shard_map/all_gather | solution.py:295
  275.2 1.0 copy-start.6
  276.2 74.9 %all-to-all-start.3 = ((f32[8,16,8,256]{3,2,1,0:T(8,128)}), f32[8,16,8,256]{3,2,1,0:T(8,128)}, u32[]{:S(2)}, u32[]{:S(2)}) async-start(f32[8,16,8,256]{3,2,1,0:T(8,128)} %bitcast.157), calls=%async_computation.5 | async-start | bytes 2097152 | tf_op jit(solution)/shard_map/all_to_all | solution.py:21
  284.4 3.0 copy-start.9
  348.9 2.2 copy-start.2
  351.1 8.5 copy-start.8
  351.1 104.5 %all-to-all-start.4 = ((f32[8,17,32,256]{3,2,1,0:T(8,128)}), f32[8,17,32,256]{3,2,1,0:T(8,128)}, u32[]{:S(2)}, u32[]{:S(2)}) async-start(f32[8,17,32,256]{3,2,1,0:T(8,128)} %copy-done.2), calls=%async_computation.6 | async-start | bytes 8912896 | tf_op jit(solution)/shard_map/all_to_all | solution.py:21
  355.8 55.6 %all-gather.9.cloned.1.call-start = ((), (), s32[]{:S(2)}) async-start(), calls=%async_computation.15 | async-start | bytes 5242880 | tf_op jit(solution)/shard_map/all_gather | solution.py:288
  455.6 2.2 copy-start.4
  477.2 104.2 %all-to-all-start.5 = ((f32[8,17,32,256]{3,2,1,0:T(8,128)}), f32[8,17,32,256]{3,2,1,0:T(8,128)}, u32[]{:S(2)}, u32[]{:S(2)}) async-start(f32[8,17,32,256]{3,2,1,0:T(8,128)} %bitcast.145), calls=%async_computation.7 | async-start | bytes 8912896 | tf_op jit(solution)/shard_map/all_to_all | solution.py:21
  481.8 286.5 %reduce-scatter.8.cloned.1.call-start = ((), (), s32[]{:S(2)}) async-start(), calls=%async_computation.13 | async-start | bytes 5242880 | tf_op jit(solution)/shard_map/reduce_scatter | solution.py:274
  715.6 2.0 copy-start.3
  717.6 50.7 %copy-start.7 = (f32[8,256,128]{2,1,0:T(8,128)S(1)}, f32[8,256,128]{2,1,0:T(8,128)}, u32[]{:S(2)}) copy-start(f32[8,256,128]{2,1,0:T(8,128)} %reduce-scatter.6.cloned.1.call-done) | copy-start | bytes 3145732
  717.6 134.5 %all-gather.11.cloned.1.call-start = ((), (), s32[]{:S(2)}) async-start(), calls=%async_computation.16 | async-start | bytes 5242880 | tf_op jit(solution)/shard_map/all_gather | solution.py:288
  852.1 4.9 copy-start.1
Sparse Core Ops, SparseCore 0:
  130.5 51.6 reduce-scatter.3
  185.9 52.6 reduce-scatter.5
  276.3 52.8 all-gather.6
  358.2 53.1 all-gather.8
  717.8 50.5 reduce-scatter.7
  801.5 50.5 all-gather.10

commit v3 on v2

--- a/solution.py
+++ b/solution.py
@@ -30,12 +30,17 @@
     return top, (values - top.astype(jnp.float32)).astype(jnp.bfloat16)
 
 
+def table_halves(table):
+    top = lax.reduce_precision(table, 8, 7)
+    return top.astype(jnp.bfloat16), (table - top).astype(jnp.bfloat16)
+
+
 def pair_dot(left, right):
     once = lambda a, b: jnp.dot(a, b, preferred_element_type=jnp.float32)
     return once(left[0], right[0]) + (once(left[0], right[1]) + once(left[1], right[0]))
 
 
-def rows_kernel(sign, values, transfer, forth_hi, forth_lo, back_hi, back_lo, out):
+def rows_kernel(sign, values, transfer, forth_hi, forth_lo, back_hi, back_lo, *outs):
     ny, nz = transfer.shape[1], transfer.shape[2] // 2
     spectrum = pair_dot((forth_hi[...], forth_lo[...]), halves(values[...].reshape(ny, 2 * nz)))
     real = spectrum[:ny, :nz] + spectrum[ny:, nz:]
@@ -47,7 +52,10 @@
     spectrum = pair_dot((back_hi[...], back_lo[...]), halves(product))
     real = spectrum[:ny, :nz] - spectrum[ny:, nz:]
     imag = spectrum[:ny, nz:] + spectrum[ny:, :nz]
-    out[...] = jnp.concatenate([real, imag], -1).reshape(out.shape)
+    lines = jnp.concatenate([real, imag], -1)
+    count = ny // len(outs)
+    for part, out in enumerate(outs):
+        out[...] = lines[part * count : (part + 1) * count].reshape(out.shape)
 
 
 def pencil_back(values, z_table, x_table):
@@ -92,7 +100,8 @@
 
 
 def weigh_kernel(values, weight, bz, bzl, bx, bxl, out):
-    rows, nz = weight.shape[0], weight.shape[2]
+    rows, nz = out.shape[0], out.shape[2]
+    weight = weight[...].reshape(out.shape)
     wide = pencil_back(values, (bz[...], bzl[...]), (bx[...], bxl[...]))
     for row in range(rows):
         out[row] = weight[row] * wide[:, row * nz : (row + 1) * nz]
@@ -108,7 +117,11 @@
         grid=(grid,),
         in_specs=specs,
         out_specs=out_spec,
-        out_shape=jax.ShapeDtypeStruct(out_shape, jnp.float32),
+        out_shape=jax.tree.map(
+            lambda shape: jax.ShapeDtypeStruct(shape, jnp.float32),
+            out_shape,
+            is_leaf=lambda leaf: isinstance(leaf, tuple),
+        ),
         compiler_params=pltpu.CompilerParams(vmem_limit_bytes=48 << 20),
     )(*operands)
 
@@ -179,14 +192,21 @@
 
         tiled = yb % 8 == 0 and yq % 8 == 0 and kx % 8 == 0 and nz % 128 == 0
         rows = 8
-        z_forth, z_back = halves(into_z), halves(from_z)
-        x_forth = halves(into_x.reshape(2 * kx, nx))
-        x_back = halves(from_x.reshape(2 * kx, nx).T)
+        parts = 2 if tiled else 1
+        z_forth, z_back = table_halves(into_z), table_halves(from_z)
+        x_forth = table_halves(into_x.reshape(2 * kx, nx))
+        x_back = table_halves(from_x.reshape(2 * kx, nx).T)
         both_y = jnp.concatenate([cy, sy], 0)
-        y_forth, y_back = halves(both_y), halves(both_y / ny)
+        y_forth, y_back = table_halves(both_y), table_halves(both_y / ny)
         y_mixed = tuple(
             table.reshape(2 * ny, blocks, views, yq).swapaxes(1, 2).reshape(2 * ny, ny)
             for table in y_forth
+        )
+        y_parted = tuple(
+            table.reshape(2, blocks, views, parts, yq // parts, ny)
+            .transpose(0, 3, 1, 2, 4, 5)
+            .reshape(2 * ny, ny)
+            for table in y_back
         )
         lines_spec = pl.BlockSpec((kx, rows, 2 * nz), lambda step: (0, step, 0))
         cells_spec = pl.BlockSpec((rows, nx, nz), lambda step: (step, 0, 0))
@@ -214,15 +234,24 @@
             )
             return lines.reshape(blocks, kb, yb, 2 * nz)
 
-        def weighed_lines(values):
+        def weighed_lines(values, part):
             if not tiled:
                 return view_weight * backward_pencil(values)
             tables = z_back + x_back
+            piece = yq // parts
+            group = rows // piece
+            weight = view_weight.reshape(views, parts, piece, nx, nz)
             return call(
-                weigh_kernel, yb // rows,
-                [lines_spec, cells_spec] + [fixed(t) for t in tables],
-                (yb, nx, nz), cells_spec,
-                (values.reshape(kx, yb, 2 * nz), view_weight) + tables,
+                weigh_kernel, yb // parts // rows,
+                [
+                    lines_spec,
+                    pl.BlockSpec(
+                        (group, 1, piece, nx, nz), lambda step: (step, part, 0, 0, 0)
+                    ),
+                ]
+                + [fixed(t) for t in tables],
+                (yb // parts, nx, nz), cells_spec,
+                (values.reshape(kx, yb // parts, 2 * nz), weight) + tables,
             )
 
         def filter_rows(values, otf, sign, gathered):
@@ -233,22 +262,28 @@
                     values = gather_rows(values)
                 real, imag = forward_rows(values)
                 otf_real, otf_imag = otf[..., :nz], sign * otf[..., nz:]
-                return backward_rows(
-                    real * otf_real - imag * otf_imag, real * otf_imag + imag * otf_real
-                )
+                return [
+                    backward_rows(
+                        real * otf_real - imag * otf_imag, real * otf_imag + imag * otf_real
+                    )
+                ]
             spec = pl.BlockSpec((blocks, 1, yb, 2 * nz), lambda step: (0, step, 0, 0))
-            taken, forth = spec, y_forth
+            taken, forth, back, count = spec, y_forth, y_parted, parts
             if gathered:
                 taken = pl.BlockSpec(
                     (views, blocks, 1, yq, 2 * nz), lambda step: (0, 0, step, 0, 0)
                 )
-                forth = y_mixed
-            tables = forth + y_back
+                forth, back, count = y_mixed, y_back, 1
+            tables = forth + back
+            out_spec = pl.BlockSpec(
+                (blocks, 1, yb // count, 2 * nz), lambda step: (0, step, 0, 0)
+            )
             return call(
                 functools.partial(rows_kernel, sign), kb,
                 [taken, pl.BlockSpec((1, ny, 2 * nz), lambda step: (step, 0, 0))]
                 + [fixed(t) for t in tables],
-                (blocks, kb, yb, 2 * nz), spec, (values, otf) + tables,
+                [(blocks, kb, yb // count, 2 * nz)] * count, [out_spec] * count,
+                (values, otf) + tables,
             )
 
         part = dot("zyx,ax->zya", stack, map_cols)
@@ -282,11 +317,13 @@
         otf = dot("kzy,zw->kyw", both, into_z)
 
         def by_planes(values):
-            return values.transpose(2, 0, 1).reshape(blocks, zb, yq, nx)
-
-        def whole_planes(values):
-            values = lax.all_gather(values, "view", axis=0)
-            return values.transpose(2, 1, 0, 3, 4).reshape(zb, ny, nx)
+            values = values.transpose(2, 0, 1).reshape(blocks, zb, values.shape[0], nx)
+            return values.swapaxes(1, 2)
+
+        def whole_planes(pieces):
+            pieces = [lax.all_gather(piece, "view", axis=0) for piece in pieces]
+            values = jnp.stack(pieces)
+            return values.transpose(4, 2, 1, 0, 3, 5).reshape(zb, ny, nx)
 
         joined = signal_part / weight_part
         spectrum = exchange(forth_lines(joined))
@@ -294,16 +331,22 @@
         planes = exchange(planes)
         spectrum = lax.all_gather(spectrum, "view", axis=0)
         products, planes = lax.optimization_barrier(
-            (filter_rows(spectrum, otf, 1.0, True), planes)
+            (filter_rows(spectrum, otf, 1.0, True)[0], planes)
         )
         products, joined_out = lax.optimization_barrier(
-            (exchange(products), whole_planes(planes))
+            (exchange(products), whole_planes([planes]))
         )
         products = exchange(ratio_lines(products))
-        products = exchange(filter_rows(products, otf, -1.0, False))
-        total = scatter(weighed_lines(products))
-        deconvolved = joined * total / weight_part
-        return joined_out, whole_planes(exchange(by_planes(deconvolved)))
+        pieces = []
+        piece = yq // parts
+        for part, lines in enumerate(filter_rows(products, otf, -1.0, False)):
+            mine = slice(part * piece, (part + 1) * piece)
+            total = scatter(weighed_lines(exchange(lines), part))
+            if pieces:
+                total, pieces[-1] = lax.optimization_barrier((total, pieces[-1]))
+            deconvolved = joined[mine] * total / weight_part[mine]
+            pieces.append(exchange(by_planes(deconvolved)))
+        return joined_out, whole_planes(pieces)
 
     return per_device
 

time: 870 us -> 862 us (level)
  waiting for transfers between devices: 522 us -> 499 us
    reduce_scatter x3 -> x4, waiting for transfers between devices: 54 us -> 30.8 us  [per_device(): lax.psum_scatter(values, 'view', scatter_dimension=0, tiled=True)]
    all_to_all x2 -> x3, blocking collectives: 134 us -> 130 us  [exchange(): return lax.all_to_all(values, 'brick', split_axis=0, concat_axis=0)]
    all_gather x2 -> x3, waiting for transfers between devices: 101 us -> 105 us  [whole_planes(): pieces = [lax.all_gather(piece, 'view', axis=0) for piece in pieces]]
    all_to_all x6 -> x7, starting transfers between devices: 29.5 us -> 33 us  [exchange(): return lax.all_to_all(values, 'brick', split_axis=0, concat_axis=0)]
    pallas_call x5 -> x6, Pallas kernels: 72.6 us -> 75.8 us  [call(): pl.pallas_call(kernel, grid=(grid,), in_specs=specs, out_specs=out_spec,...]
    all_to_all x6 -> x7, waiting for transfers between devices: 329 us -> 326 us  [exchange(): return lax.all_to_all(values, 'brick', split_axis=0, concat_axis=0)]
  transfers between devices with their start and end apart: 12 -> 15, of which waited for: 10 -> 11; matrix products, arithmetic and copies ran while one was open for 6% -> 7% of each run, Pallas kernels for 2% -> 3%
where the time goes in v3:
time: 862 us; the launch traced here: 855 us
  waiting for transfers between devices  499 us (58%)
  blocking collectives  130 us (15%)
  Pallas kernels  75.8 us (9%)
  local copies, waits for them, and re-layouts  42.3 us (5%)
  matrix products  38.2 us (4%)
  starting transfers between devices  33.7 us (4%)
  other arithmetic  21.2 us (2%)
  between operations  14.8 us (2%)
    all_to_all x7, waiting for transfers between devices, exchange(): return lax.all_to_all(values, 'brick', split_axis=0, concat_axis=0)  326 us
    all_to_all x3, blocking collectives, exchange(): return lax.all_to_all(values, 'brick', split_axis=0, concat_axis=0)  130 us
    all_gather x3, waiting for transfers between devices, whole_planes(): pieces = [lax.all_gather(piece, 'view', axis=0) for piece in pieces]  105 us
    pallas_call x6, Pallas kernels, call(): pl.pallas_call(kernel, grid=(grid,), in_specs=specs, out_specs=out_spec,...  75.8 us
    dot_general x10, matrix products, dot(): return jnp.einsum(form, left, right, precision=exact)  38.2 us
    all_gather x1, waiting for transfers between devices, per_device(): spectrum = lax.all_gather(spectrum, 'view', axis=0)  36 us
    all_to_all x7, starting transfers between devices, exchange(): return lax.all_to_all(values, 'brick', split_axis=0, concat_axis=0)  33 us
    reduce_scatter x4, waiting for transfers between devices, per_device(): lax.psum_scatter(values, 'view', scatter_dimension=0, tiled=True)  30.8 us
  transfers between devices with their start and end apart: 15, of which 11 were waited for; matrix products, arithmetic and copies ran while one was open for 7% of the time, Pallas kernels for 3%

profile of v3, /device:TPU:0, one launch (start us, length us, event | category | flops | bytes accessed | tf_op | source)
XLA Modules:
  0.0 855.1 jit_solution(11347986453585747137)
XLA Ops:
  7.2 0.9 copy-done
  8.1 4.0 fusion.4
  12.2 2.0 fusion.52
  14.2 4.4 copy.88
  18.6 6.3 all-to-all-start
  26.0 4.9 fusion.24
  30.9 2.5 fusion.7
  33.4 2.5 fusion.9
  36.0 2.8 fusion.21
  38.8 2.8 fusion.15
  41.5 2.6 fusion.18
  44.1 2.6 maximum_bitcast_fusion
  46.7 72.4 %all-to-all-done = f32[8,32,16,256]{3,2,1,0:T(8,128)} async-done(((f32[8,32,16,256]{3,2,1,0:T(8,128)}), f32[8,32,16,256]{3,2,1,0:T(8,128)}, u32[]{:S(2)}, u32[]{:S(2)}) %all-to-all-start) | async-done | bytes 4194336 | tf_op jit(solution)/shard_map/all_to_all | solution.py:21
  119.1 2.8 copy.95
  121.9 8.4 select_add_fusion
  131.1 4.6 all-to-all-start.1
  135.7 2.0 fusion.106
  137.7 1.9 fusion.105
  139.6 2.0 fusion.104
  142.5 1.0 pad_maximum_fusion.4
  143.6 91.7 %all-to-all-done.1 = f32[8,17,2,16,256]{4,3,2,1,0:T(8,128)} async-done(((f32[8,17,2,16,256]{4,3,2,1,0:T(8,128)}), f32[8,17,2,16,256]{4,3,2,1,0:T(8,128)}, u32[]{:S(2)}, u32[]{:S(2)}) %all-to-all-start.1) | async-done | bytes 4456480 | tf_op jit(solution)/shard_map/all_to_all | solution.py:21
  235.3 3.3 reduce-scatter.7.cloned.1.call-done
  238.6 1.7 div.33.values
  240.3 2.2 shard_map.86
  242.5 4.6 all-to-all-start.2
  247.2 1.4 copy.97
  248.6 26.6 %all-to-all-done.2 = f32[8,17,8,256]{3,2,1,0:T(8,128)S(1)} async-done(((f32[8,17,8,256]{3,2,1,0:T(8,128)}), f32[8,17,8,256]{3,2,1,0:T(8,128)S(1)}, u32[]{:S(2)}, u32[]{:S(2)}) %all-to-all-start.2) | async-done | bytes 1114144 | tf_op jit(solution)/shard_map/all_to_all | solution.py:21
  275.2 1.0 copy-done.6
  276.2 4.7 all-to-all-start.3
  281.1 1.1 fusion.85
  282.5 1.0 fusion.86
  283.6 1.0 fusion.36
  284.5 2.9 copy.98
  287.5 5.7 fusion.135.transfer
  293.2 36.0 %all-gather.9.cloned.1.call-done = f32[32,17,8,256]{3,2,1,0:T(8,128)} async-done(((f32[8,17,8,256]{3,2,1,0:T(8,128)}), f32[32,17,8,256]{3,2,1,0:T(8,128)}) %all-gather.9.cloned.1.call-update) | async-done | bytes 4456464 | tf_op jit(solution)/shard_map/all_gather | solution.py:332
  329.2 19.8 %shard_map.87 = f32[8,17,32,256]{3,2,1,0:T(8,128)S(1)} custom-call(f32[4,8,17,8,256]{4,3,2,1,0:T(8,128)} %bitcast.150, f32[17,256,256]{2,1,0:T(8,128)} %fusion.135.transfer, bf16[512,256]{1,0:T(8,128)(2,1)S(1)} %copy.100.forth_hi, bf16[512,256]{1,0:T(8,128)(2,1)S(1)} %copy.101.forth_lo, bf16[512,256]{1,0:T(8,128)(2,1)S(1)} %get-tuple-element.37.back_hi, ...), custom_call_target="tpu_custom_call" | custom-call | tf_op jit(solution)/shard_map/pallas_call | solution.py:115
  348.9 2.1 copy-done.2
  351.1 4.6 all-to-all-start.4
  355.9 2.5 copy.102
  359.4 52.5 %all-gather.11.cloned.1.call-done = f32[32,8,16,256]{3,2,1,0:T(8,128)} async-done(((f32[8,8,16,256]{3,2,1,0:T(8,128)}), f32[32,8,16,256]{3,2,1,0:T(8,128)}) %all-gather.11.cloned.1.call-update) | async-done | bytes 4194320 | tf_op jit(solution)/shard_map/all_gather | solution.py:324
  411.9 6.6 copy.103
  418.5 36.9 %all-to-all-done.4 = f32[8,17,32,256]{3,2,1,0:T(8,128)} async-done(((f32[8,17,32,256]{3,2,1,0:T(8,128)}), f32[8,17,32,256]{3,2,1,0:T(8,128)}, u32[]{:S(2)}, u32[]{:S(2)}) %all-to-all-start.4) | async-done | bytes 4456480 | tf_op jit(solution)/shard_map/all_to_all | solution.py:21
  455.4 2.2 copy-done.3
  457.6 19.5 %shard_map.88 = f32[136,32,256]{2,1,0:T(8,128)} custom-call(f32[136,32,256]{2,1,0:T(8,128)} %bitcast.44.values, f32[32,256,128]{2,1,0:T(8,128)S(1)} %copy-done.3, bf16[256,256]{1,0:T(8,128)(2,1)S(1)} %get-tuple-element.48.bz, bf16[256,256]{1,0:T(8,128)(2,1)S(1)} %get-tuple-element.47.bzl, bf16[256,272]{1,0:T(8,128)(2,1)S(1)} %get-tuple-element.44.bx, ...), custom_call_target="tpu_custom_call" | custom-call | tf_op jit(solution)/shard_map/pallas_call | solution.py:115
  477.1 4.7 all-to-all-start.5
  482.7 98.7 %all-to-all-done.5.values = f32[8,17,32,256]{3,2,1,0:T(8,128)} async-done(((f32[8,17,32,256]{3,2,1,0:T(8,128)}), f32[8,17,32,256]{3,2,1,0:T(8,128)}, u32[]{:S(2)}, u32[]{:S(2)}) %all-to-all-start.5) | async-done | bytes 4456480 | tf_op jit(solution)/shard_map/all_to_all | solution.py:21
  581.4 20.0 %shard_map.89 = (f32[8,17,16,256]{3,2,1,0:T(8,128)S(1)}, f32[8,17,16,256]{3,2,1,0:T(8,128)S(1)}) custom-call(f32[8,17,32,256]{3,2,1,0:T(8,128)} %all-to-all-done.5.values, f32[17,256,256]{2,1,0:T(8,128)} %fusion.135.transfer, bf16[512,256]{1,0:T(8,128)(2,1)S(1)} %get-tuple-element.40.forth_hi, bf16[512,256]{1,0:T(8,128)(2,1)S(1)} %get-tuple-element.39.forth_lo, ...), custom_call_target="tpu_custom_call" | custom-call | tf_op jit(solution)/shard_map/pallas_call | solution.py:115
  601.5 1.4 copy-done.4
  602.9 54.3 %all_to_all.50 = f32[8,17,16,256]{3,2,1,0:T(8,128)S(1)} all-to-all(f32[8,17,16,256]{3,2,1,0:T(8,128)S(1)} %get-tuple-element.29), channel_id=1, replica_groups=mesh['view'=4,'brick'=8] {'brick'}, dimensions={0} | all-to-all | bytes 4456448 | tf_op jit(solution)/shard_map/all_to_all | solution.py:21
  657.2 7.1 shard_map.91
  664.3 55.6 %all_to_all.51 = f32[8,17,16,256]{3,2,1,0:T(8,128)S(1)} all-to-all(f32[8,17,16,256]{3,2,1,0:T(8,128)} %copy-done.4), channel_id=1, replica_groups=mesh['view'=4,'brick'=8] {'brick'}, dimensions={0} | all-to-all | bytes 4456448 | tf_op jit(solution)/shard_map/all_to_all | solution.py:21
  720.0 7.2 shard_map.90
  727.2 1.1 fusion.34
  728.5 0.8 copy.110
  729.4 3.5 all-to-all-start.8
  732.9 27.5 %reduce-scatter.9.cloned.1.call-done = f32[4,256,128]{2,1,0:T(8,128)} async-done(((f32[16,256,128]{2,1,0:T(8,128)}), f32[4,256,128]{2,1,0:T(8,128)}) %reduce-scatter.9.cloned.1.call-update) | async-done | bytes 524304 | tf_op jit(solution)/shard_map/reduce_scatter | solution.py:309
  760.4 0.8 copy-done.8
  761.3 1.1 fusion.32
  762.7 19.9 %all_to_all.52 = f32[8,4,16,256]{3,2,1,0:T(8,128)} all-to-all(f32[8,4,16,256]{3,2,1,0:T(8,128)S(1)} %copy.112), channel_id=1, replica_groups=mesh['view'=4,'brick'=8] {'brick'}, dimensions={0} | all-to-all | bytes 1048576 | tf_op jit(solution)/shard_map/all_to_all | solution.py:21
  782.6 15.6 %all-gather.13.cloned.1.call-done = f32[32,4,16,256]{3,2,1,0:T(8,128)} async-done(((f32[8,4,16,256]{3,2,1,0:T(8,128)}), f32[32,4,16,256]{3,2,1,0:T(8,128)}) %all-gather.13.cloned.1.call-update) | async-done | bytes 2097168 | tf_op jit(solution)/shard_map/all_gather | solution.py:324
  798.2 37.2 %all-gather.15.cloned.1.call-done = f32[32,4,16,256]{3,2,1,0:T(8,128)} async-done(((f32[8,4,16,256]{3,2,1,0:T(8,128)}), f32[32,4,16,256]{3,2,1,0:T(8,128)}) %all-gather.15.cloned.1.call-update) | async-done | bytes 2097168 | tf_op jit(solution)/shard_map/all_gather | solution.py:324
  835.4 2.7 maximum_bitcast_fusion.1
  838.1 4.7 copy.113
  842.8 5.3 reshape.403
  (67 shorter events, 6.0 us)
Async XLA Ops:
  7.2 1.0 copy-start
  7.2 5.0 copy-start.11
  18.6 100.4 %all-to-all-start = ((f32[8,32,16,256]{3,2,1,0:T(8,128)}), f32[8,32,16,256]{3,2,1,0:T(8,128)}, u32[]{:S(2)}, u32[]{:S(2)}) async-start(f32[8,32,16,256]{3,2,1,0:T(8,128)} %copy.88), calls=%async_computation | async-start | bytes 8388608 | tf_op jit(solution)/shard_map/all_to_all | solution.py:21
  25.0 210.4 %reduce-scatter.5.cloned.1.call-start = ((), (), s32[]{:S(2)}) async-start(), calls=%async_computation.14 | async-start | bytes 5242880 | tf_op jit(solution)/shard_map/reduce_scatter | solution.py:309
  30.9 5.0 copy-start.5
  46.7 75.2 %copy-start.12 = (f32[1,128,128]{2,1,0:T(8,128)S(1)}, f32[1,128,128]{2,1,0:T(8,128)}, u32[]{:S(2)}) copy-start(f32[1,128,128]{2,1,0:T(8,128)} %param.9) | copy-start | bytes 196612
  130.3 108.3 %reduce-scatter.7.cloned.1.call-start = ((), (), s32[]{:S(2)}) async-start(), calls=%async_computation.15 | async-start | bytes 5242880 | tf_op jit(solution)/shard_map/reduce_scatter | solution.py:309
  131.1 104.2 %all-to-all-start.1 = ((f32[8,17,2,16,256]{4,3,2,1,0:T(8,128)}), f32[8,17,2,16,256]{4,3,2,1,0:T(8,128)}, u32[]{:S(2)}, u32[]{:S(2)}) async-start(f32[8,17,2,16,256]{4,3,2,1,0:T(8,128)} %maximum_bitcast_fusion), calls=%async_computation.3 | async-start | bytes 8912896 | tf_op jit(solution)/shard_map/all_to_all | solution.py:21
  242.5 32.6 %all-to-all-start.2 = ((f32[8,17,8,256]{3,2,1,0:T(8,128)}), f32[8,17,8,256]{3,2,1,0:T(8,128)S(1)}, u32[]{:S(2)}, u32[]{:S(2)}) async-start(f32[8,17,8,256]{3,2,1,0:T(8,128)} %bitcast.30), calls=%async_computation.4 | async-start | bytes 2228224 | tf_op jit(solution)/shard_map/all_to_all | solution.py:21
  247.2 82.0 %all-gather.9.cloned.1.call-start = ((), (), s32[]{:S(2)}) async-start(), calls=%async_computation.18 | async-start | bytes 5570560 | tf_op jit(solution)/shard_map/all_gather | solution.py:332
  275.2 1.0 copy-start.6
  276.2 74.9 %all-to-all-start.3 = ((f32[8,8,16,256]{3,1,2,0:T(8,128)}), f32[8,8,16,256]{3,1,2,0:T(8,128)}, u32[]{:S(2)}, u32[]{:S(2)}) async-start(f32[8,8,16,256]{3,1,2,0:T(8,128)} %bitcast.153), calls=%async_computation.5 | async-start | bytes 2097152 | tf_op jit(solution)/shard_map/all_to_all | solution.py:21
  348.9 2.2 copy-start.2
  351.1 104.3 %all-to-all-start.4 = ((f32[8,17,32,256]{3,2,1,0:T(8,128)}), f32[8,17,32,256]{3,2,1,0:T(8,128)}, u32[]{:S(2)}, u32[]{:S(2)}) async-start(f32[8,17,32,256]{3,2,1,0:T(8,128)} %copy-done.2), calls=%async_computation.6 | async-start | bytes 8912896 | tf_op jit(solution)/shard_map/all_to_all | solution.py:21
  355.7 3.6 copy-start.10
  355.7 56.2 %all-gather.11.cloned.1.call-start = ((), (), s32[]{:S(2)}) async-start(), calls=%async_computation.19 | async-start | bytes 5242880 | tf_op jit(solution)/shard_map/all_gather | solution.py:324
  455.4 2.2 copy-start.3
  477.1 4.8 copy-start.9
  477.1 104.4 %all-to-all-start.5 = ((f32[8,17,32,256]{3,2,1,0:T(8,128)}), f32[8,17,32,256]{3,2,1,0:T(8,128)}, u32[]{:S(2)}, u32[]{:S(2)}) async-start(f32[8,17,32,256]{3,2,1,0:T(8,128)} %bitcast.144), calls=%async_computation.7 | async-start | bytes 8912896 | tf_op jit(solution)/shard_map/all_to_all | solution.py:21
  481.8 245.4 %reduce-scatter.11.cloned.1.call-start = ((), (), s32[]{:S(2)}) async-start(), calls=%async_computation.17 | async-start | bytes 2621440 | tf_op jit(solution)/shard_map/reduce_scatter | solution.py:309
  601.5 1.4 copy-start.4
  664.3 96.1 %reduce-scatter.9.cloned.1.call-start = ((), (), s32[]{:S(2)}) async-start(), calls=%async_computation.16 | async-start | bytes 2621440 | tf_op jit(solution)/shard_map/reduce_scatter | solution.py:309
  720.0 7.2 copy-start.7
  729.4 31.1 %all-to-all-start.8 = ((f32[8,4,16,256]{3,2,1,0:T(8,128)}), f32[8,4,16,256]{3,2,1,0:T(8,128)S(1)}, u32[]{:S(2)}, u32[]{:S(2)}) async-start(f32[8,4,16,256]{3,2,1,0:T(8,128)} %copy.110), calls=%async_computation.12 | async-start | bytes 1048576 | tf_op jit(solution)/shard_map/all_to_all | solution.py:21
  732.9 65.3 %all-gather.13.cloned.1.call-start = ((), (), s32[]{:S(2)}) async-start(), calls=%async_computation.20 | async-start | bytes 2621440 | tf_op jit(solution)/shard_map/all_gather | solution.py:324
  760.4 0.8 copy-start.8
  761.3 74.1 %all-gather.15.cloned.1.call-start = ((), (), s32[]{:S(2)}) async-start(), calls=%async_computation.21 | async-start | bytes 2621440 | tf_op jit(solution)/shard_map/all_gather | solution.py:324
  838.1 10.0 %copy-start.1 = (f32[1,256,256]{2,1,0:T(8,128)S(1)}, f32[1,256,256]{2,1,0:T(8,128)}, u32[]{:S(2)}) copy-start(f32[1,256,256]{2,1,0:T(8,128)} %param.11) | copy-start | bytes 786436
Sparse Core Ops, SparseCore 0:
  130.5 51.6 reduce-scatter.4
  185.9 52.6 reduce-scatter.6
  276.3 52.8 all-gather.8
  358.7 53.1 all-gather.10
  664.4 33.1 reduce-scatter.10
  727.3 33.1 reduce-scatter.8
  762.9 35.2 all-gather.12
  800.0 35.2 all-gather.14

commit v4 on v3

--- a/solution.py
+++ b/solution.py
@@ -339,9 +339,13 @@
         products = exchange(ratio_lines(products))
         pieces = []
         piece = yq // parts
+        weighed = None
         for part, lines in enumerate(filter_rows(products, otf, -1.0, False)):
             mine = slice(part * piece, (part + 1) * piece)
-            total = scatter(weighed_lines(exchange(lines), part))
+            if weighed is not None:
+                _, lines = lax.optimization_barrier((weighed, lines))
+            weighed = weighed_lines(exchange(lines), part)
+            total = scatter(weighed)
             if pieces:
                 total, pieces[-1] = lax.optimization_barrier((total, pieces[-1]))
             deconvolved = joined[mine] * total / weight_part[mine]

time: 862 us -> 861 us (level)
  blocking collectives: 130 us -> 148 us
  waiting for transfers between devices: 499 us -> 484 us
    all_to_all x3 -> x4, blocking collectives: 130 us -> 148 us  [exchange(): return lax.all_to_all(values, 'brick', split_axis=0, concat_axis=0)]
    reduce_scatter x4, waiting for transfers between devices: 30.8 us -> 16.5 us  [per_device(): lax.psum_scatter(values, 'view', scatter_dimension=0, tiled=True)]
    all_to_all x7 -> x6, starting transfers between devices: 33 us -> 29.2 us  [exchange(): return lax.all_to_all(values, 'brick', split_axis=0, concat_axis=0)]
    all_to_all x7 -> x6, waiting for transfers between devices: 326 us -> 325 us  [exchange(): return lax.all_to_all(values, 'brick', split_axis=0, concat_axis=0)]
  transfers between devices with their start and end apart: 15 -> 14, of which waited for: 11 -> 11; matrix products, arithmetic and copies ran while one was open for 7% -> 7% of each run, Pallas kernels for 3% -> 3%
where the time goes in v4:
time: 861 us; the launch traced here: 855 us
  waiting for transfers between devices  484 us (56%)
  blocking collectives  148 us (17%)
  Pallas kernels  75.7 us (9%)
  local copies, waits for them, and re-layouts  41.8 us (5%)
  matrix products  38.2 us (4%)
  starting transfers between devices  30.3 us (4%)
  other arithmetic  21.5 us (2%)
  between operations  14.7 us (2%)
    all_to_all x6, waiting for transfers between devices, exchange(): return lax.all_to_all(values, 'brick', split_axis=0, concat_axis=0)  325 us
    all_to_all x4, blocking collectives, exchange(): return lax.all_to_all(values, 'brick', split_axis=0, concat_axis=0)  148 us
    all_gather x3, waiting for transfers between devices, whole_planes(): pieces = [lax.all_gather(piece, 'view', axis=0) for piece in pieces]  105 us
    pallas_call x6, Pallas kernels, call(): pl.pallas_call(kernel, grid=(grid,), in_specs=specs, out_specs=out_spec,...  75.7 us
    dot_general x10, matrix products, dot(): return jnp.einsum(form, left, right, precision=exact)  38.2 us
    all_gather x1, waiting for transfers between devices, per_device(): spectrum = lax.all_gather(spectrum, 'view', axis=0)  36.1 us
    all_to_all x6, starting transfers between devices, exchange(): return lax.all_to_all(values, 'brick', split_axis=0, concat_axis=0)  29.2 us
  transfers between devices with their start and end apart: 14, of which 11 were waited for; matrix products, arithmetic and copies ran while one was open for 7% of the time, Pallas kernels for 3%

profile of v4, /device:TPU:0, one launch (start us, length us, event | category | flops | bytes accessed | tf_op | source)
XLA Modules:
  0.0 854.5 jit_solution(13538019057869833826)
XLA Ops:
  7.2 0.9 copy-done
  8.1 4.0 fusion.4
  12.2 2.1 fusion.52
  14.2 4.4 copy.88
  18.6 6.3 all-to-all-start
  25.6 0.8 dynamic-slice_bitcast_fusion
  26.4 4.9 fusion.24
  31.3 2.5 fusion.7
  33.8 2.5 fusion.9
  36.4 2.8 fusion.21
  39.1 2.7 fusion.15
  41.9 2.6 fusion.18
  44.4 2.6 maximum_bitcast_fusion
  47.1 72.1 %all-to-all-done = f32[8,32,16,256]{3,2,1,0:T(8,128)} async-done(((f32[8,32,16,256]{3,2,1,0:T(8,128)}), f32[8,32,16,256]{3,2,1,0:T(8,128)}, u32[]{:S(2)}, u32[]{:S(2)}) %all-to-all-start) | async-done | bytes 4194336 | tf_op jit(solution)/shard_map/all_to_all | solution.py:21
  119.1 2.8 copy.95
  121.9 8.4 select_add_fusion
  131.1 4.6 all-to-all-start.1
  135.7 2.0 fusion.106
  137.7 1.9 fusion.105
  139.6 2.0 fusion.104
  142.5 1.0 pad_maximum_fusion.4
  143.6 91.7 %all-to-all-done.1 = f32[8,17,2,16,256]{4,3,2,1,0:T(8,128)} async-done(((f32[8,17,2,16,256]{4,3,2,1,0:T(8,128)}), f32[8,17,2,16,256]{4,3,2,1,0:T(8,128)}, u32[]{:S(2)}, u32[]{:S(2)}) %all-to-all-start.1) | async-done | bytes 4456480 | tf_op jit(solution)/shard_map/all_to_all | solution.py:21
  235.3 3.3 reduce-scatter.7.cloned.1.call-done
  238.7 1.7 div.33.values
  240.4 2.2 shard_map.86
  242.6 4.6 all-to-all-start.2
  247.2 1.4 copy.97
  248.6 26.5 %all-to-all-done.2 = f32[8,17,8,256]{3,2,1,0:T(8,128)S(1)} async-done(((f32[8,17,8,256]{3,2,1,0:T(8,128)}), f32[8,17,8,256]{3,2,1,0:T(8,128)S(1)}, u32[]{:S(2)}, u32[]{:S(2)}) %all-to-all-start.2) | async-done | bytes 1114144 | tf_op jit(solution)/shard_map/all_to_all | solution.py:21
  275.2 1.0 copy-done.6
  276.2 4.5 all-to-all-start.3
  280.9 1.1 fusion.85
  282.4 1.0 fusion.86
  283.4 1.0 fusion.36
  284.4 2.9 copy.98
  287.3 5.7 fusion.135.transfer
  293.0 36.1 %all-gather.9.cloned.1.call-done = f32[32,17,8,256]{3,2,1,0:T(8,128)} async-done(((f32[8,17,8,256]{3,2,1,0:T(8,128)}), f32[32,17,8,256]{3,2,1,0:T(8,128)}) %all-gather.9.cloned.1.call-update) | async-done | bytes 4456464 | tf_op jit(solution)/shard_map/all_gather | solution.py:332
  329.2 19.8 %shard_map.87 = f32[8,17,32,256]{3,2,1,0:T(8,128)S(1)} custom-call(f32[4,8,17,8,256]{4,3,2,1,0:T(8,128)} %bitcast.150, f32[17,256,256]{2,1,0:T(8,128)} %fusion.135.transfer, bf16[512,256]{1,0:T(8,128)(2,1)S(1)} %copy.100.forth_hi, bf16[512,256]{1,0:T(8,128)(2,1)S(1)} %copy.101.forth_lo, bf16[512,256]{1,0:T(8,128)(2,1)S(1)} %get-tuple-element.39.back_hi, ...), custom_call_target="tpu_custom_call" | custom-call | tf_op jit(solution)/shard_map/pallas_call | solution.py:115
  349.0 2.2 copy-done.2
  351.1 4.6 all-to-all-start.4
  356.0 2.5 copy.102
  359.5 52.4 %all-gather.11.cloned.1.call-done = f32[32,8,16,256]{3,2,1,0:T(8,128)} async-done(((f32[8,8,16,256]{3,2,1,0:T(8,128)}), f32[32,8,16,256]{3,2,1,0:T(8,128)}) %all-gather.11.cloned.1.call-update) | async-done | bytes 4194320 | tf_op jit(solution)/shard_map/all_gather | solution.py:324
  411.9 6.6 copy.103
  418.5 36.9 %all-to-all-done.4 = f32[8,17,32,256]{3,2,1,0:T(8,128)} async-done(((f32[8,17,32,256]{3,2,1,0:T(8,128)}), f32[8,17,32,256]{3,2,1,0:T(8,128)}, u32[]{:S(2)}, u32[]{:S(2)}) %all-to-all-start.4) | async-done | bytes 4456480 | tf_op jit(solution)/shard_map/all_to_all | solution.py:21
  455.5 2.2 copy-done.3
  457.6 19.5 %shard_map.88 = f32[136,32,256]{2,1,0:T(8,128)} custom-call(f32[136,32,256]{2,1,0:T(8,128)} %bitcast.44.values, f32[32,256,128]{2,1,0:T(8,128)S(1)} %copy-done.3, bf16[256,256]{1,0:T(8,128)(2,1)S(1)} %get-tuple-element.50.bz, bf16[256,256]{1,0:T(8,128)(2,1)S(1)} %get-tuple-element.49.bzl, bf16[256,272]{1,0:T(8,128)(2,1)S(1)} %get-tuple-element.46.bx, ...), custom_call_target="tpu_custom_call" | custom-call | tf_op jit(solution)/shard_map/pallas_call | solution.py:115
  477.1 4.6 all-to-all-start.5
  481.8 1.2 div.41
  483.6 97.7 %all-to-all-done.5.values = f32[8,17,32,256]{3,2,1,0:T(8,128)} async-done(((f32[8,17,32,256]{3,2,1,0:T(8,128)}), f32[8,17,32,256]{3,2,1,0:T(8,128)}, u32[]{:S(2)}, u32[]{:S(2)}) %all-to-all-start.5) | async-done | bytes 4456480 | tf_op jit(solution)/shard_map/all_to_all | solution.py:21
  581.3 20.0 %shard_map.89 = (f32[8,17,16,256]{3,2,1,0:T(8,128)S(1)}, f32[8,17,16,256]{3,2,1,0:T(8,128)S(1)}) custom-call(f32[8,17,32,256]{3,2,1,0:T(8,128)} %all-to-all-done.5.values, f32[17,256,256]{2,1,0:T(8,128)} %fusion.135.transfer, bf16[512,256]{1,0:T(8,128)(2,1)S(1)} %get-tuple-element.42.forth_hi, bf16[512,256]{1,0:T(8,128)(2,1)S(1)} %get-tuple-element.41.forth_lo, ...), custom_call_target="tpu_custom_call" | custom-call | tf_op jit(solution)/shard_map/pallas_call | solution.py:115
  601.4 1.4 copy-done.4
  602.8 54.3 %all_to_all.50 = f32[8,17,16,256]{3,2,1,0:T(8,128)S(1)} all-to-all(f32[8,17,16,256]{3,2,1,0:T(8,128)S(1)} %get-tuple-element.29), channel_id=1, replica_groups=mesh['view'=4,'brick'=8] {'brick'}, dimensions={0} | all-to-all | bytes 4456448 | tf_op jit(solution)/shard_map/all_to_all | solution.py:21
  657.1 7.1 shard_map.90
  664.2 55.9 %all_to_all.51 = f32[8,17,16,256]{3,2,1,0:T(8,128)S(1)} all-to-all(f32[8,17,16,256]{3,2,1,0:T(8,128)} %copy-done.4), channel_id=1, replica_groups=mesh['view'=4,'brick'=8] {'brick'}, dimensions={0} | all-to-all | bytes 4456448 | tf_op jit(solution)/shard_map/all_to_all | solution.py:21
  720.1 7.1 shard_map.91
  727.3 1.3 fusion.34
  728.9 18.4 %all_to_all.52 = f32[8,4,16,256]{3,2,1,0:T(8,128)} all-to-all(f32[8,4,16,256]{3,2,1,0:T(8,128)S(1)} %copy.110), channel_id=1, replica_groups=mesh['view'=4,'brick'=8] {'brick'}, dimensions={0} | all-to-all | bytes 1048576 | tf_op jit(solution)/shard_map/all_to_all | solution.py:21
  747.3 13.2 %reduce-scatter.9.cloned.1.call-done = f32[4,256,128]{2,1,0:T(8,128)} async-done(((f32[16,256,128]{2,1,0:T(8,128)}), f32[4,256,128]{2,1,0:T(8,128)}) %reduce-scatter.9.cloned.1.call-update) | async-done | bytes 524304 | tf_op jit(solution)/shard_map/reduce_scatter | solution.py:309
  760.6 1.1 fusion.32
  762.0 19.9 %all_to_all.53 = f32[8,4,16,256]{3,2,1,0:T(8,128)} all-to-all(f32[8,4,16,256]{3,2,1,0:T(8,128)S(1)} %copy.112), channel_id=1, replica_groups=mesh['view'=4,'brick'=8] {'brick'}, dimensions={0} | all-to-all | bytes 1048576 | tf_op jit(solution)/shard_map/all_to_all | solution.py:21
  781.8 15.8 %all-gather.13.cloned.1.call-done = f32[32,4,16,256]{3,2,1,0:T(8,128)} async-done(((f32[8,4,16,256]{3,2,1,0:T(8,128)}), f32[32,4,16,256]{3,2,1,0:T(8,128)}) %all-gather.13.cloned.1.call-update) | async-done | bytes 2097168 | tf_op jit(solution)/shard_map/all_gather | solution.py:324
  797.7 37.2 %all-gather.15.cloned.1.call-done = f32[32,4,16,256]{3,2,1,0:T(8,128)} async-done(((f32[8,4,16,256]{3,2,1,0:T(8,128)}), f32[32,4,16,256]{3,2,1,0:T(8,128)}) %all-gather.15.cloned.1.call-update) | async-done | bytes 2097168 | tf_op jit(solution)/shard_map/all_gather | solution.py:324
  834.9 2.7 maximum_bitcast_fusion.1
  837.6 4.7 copy.113
  842.3 5.3 reshape.403
  (62 shorter events, 5.5 us)
Async XLA Ops:
  7.2 1.0 copy-start
  7.2 5.0 copy-start.9
  18.6 100.5 %all-to-all-start = ((f32[8,32,16,256]{3,2,1,0:T(8,128)}), f32[8,32,16,256]{3,2,1,0:T(8,128)}, u32[]{:S(2)}, u32[]{:S(2)}) async-start(f32[8,32,16,256]{3,2,1,0:T(8,128)} %copy.88), calls=%async_computation | async-start | bytes 8388608 | tf_op jit(solution)/shard_map/all_to_all | solution.py:21
  25.0 210.3 %reduce-scatter.5.cloned.1.call-start = ((), (), s32[]{:S(2)}) async-start(), calls=%async_computation.14 | async-start | bytes 5242880 | tf_op jit(solution)/shard_map/reduce_scatter | solution.py:309
  31.3 5.0 copy-start.5
  47.1 74.9 %copy-start.10 = (f32[1,128,128]{2,1,0:T(8,128)S(1)}, f32[1,128,128]{2,1,0:T(8,128)}, u32[]{:S(2)}) copy-start(f32[1,128,128]{2,1,0:T(8,128)} %param.9) | copy-start | bytes 196612
  130.4 108.3 %reduce-scatter.7.cloned.1.call-start = ((), (), s32[]{:S(2)}) async-start(), calls=%async_computation.15 | async-start | bytes 5242880 | tf_op jit(solution)/shard_map/reduce_scatter | solution.py:309
  131.1 104.2 %all-to-all-start.1 = ((f32[8,17,2,16,256]{4,3,2,1,0:T(8,128)}), f32[8,17,2,16,256]{4,3,2,1,0:T(8,128)}, u32[]{:S(2)}, u32[]{:S(2)}) async-start(f32[8,17,2,16,256]{4,3,2,1,0:T(8,128)} %maximum_bitcast_fusion), calls=%async_computation.3 | async-start | bytes 8912896 | tf_op jit(solution)/shard_map/all_to_all | solution.py:21
  242.6 32.6 %all-to-all-start.2 = ((f32[8,17,8,256]{3,2,1,0:T(8,128)}), f32[8,17,8,256]{3,2,1,0:T(8,128)S(1)}, u32[]{:S(2)}, u32[]{:S(2)}) async-start(f32[8,17,8,256]{3,2,1,0:T(8,128)} %bitcast.30), calls=%async_computation.4 | async-start | bytes 2228224 | tf_op jit(solution)/shard_map/all_to_all | solution.py:21
  247.2 82.0 %all-gather.9.cloned.1.call-start = ((), (), s32[]{:S(2)}) async-start(), calls=%async_computation.18 | async-start | bytes 5570560 | tf_op jit(solution)/shard_map/all_gather | solution.py:332
  275.2 1.0 copy-start.6
  276.2 74.9 %all-to-all-start.3 = ((f32[8,8,16,256]{3,1,2,0:T(8,128)}), f32[8,8,16,256]{3,1,2,0:T(8,128)}, u32[]{:S(2)}, u32[]{:S(2)}) async-start(f32[8,8,16,256]{3,1,2,0:T(8,128)} %bitcast.153), calls=%async_computation.5 | async-start | bytes 2097152 | tf_op jit(solution)/shard_map/all_to_all | solution.py:21
  348.9 2.2 copy-start.2
  351.1 104.3 %all-to-all-start.4 = ((f32[8,17,32,256]{3,2,1,0:T(8,128)}), f32[8,17,32,256]{3,2,1,0:T(8,128)}, u32[]{:S(2)}, u32[]{:S(2)}) async-start(f32[8,17,32,256]{3,2,1,0:T(8,128)} %copy-done.2), calls=%async_computation.6 | async-start | bytes 8912896 | tf_op jit(solution)/shard_map/all_to_all | solution.py:21
  355.7 3.6 copy-start.8
  355.7 56.2 %all-gather.11.cloned.1.call-start = ((), (), s32[]{:S(2)}) async-start(), calls=%async_computation.19 | async-start | bytes 5242880 | tf_op jit(solution)/shard_map/all_gather | solution.py:324
  455.5 2.2 copy-start.3
  477.1 104.2 %all-to-all-start.5 = ((f32[8,17,32,256]{3,2,1,0:T(8,128)}), f32[8,17,32,256]{3,2,1,0:T(8,128)}, u32[]{:S(2)}, u32[]{:S(2)}) async-start(f32[8,17,32,256]{3,2,1,0:T(8,128)} %bitcast.144), calls=%async_computation.7 | async-start | bytes 8912896 | tf_op jit(solution)/shard_map/all_to_all | solution.py:21
  481.7 245.6 %reduce-scatter.11.cloned.1.call-start = ((), (), s32[]{:S(2)}) async-start(), calls=%async_computation.17 | async-start | bytes 2621440 | tf_op jit(solution)/shard_map/reduce_scatter | solution.py:309
  601.4 1.4 copy-start.4
  664.2 96.3 %reduce-scatter.9.cloned.1.call-start = ((), (), s32[]{:S(2)}) async-start(), calls=%async_computation.16 | async-start | bytes 2621440 | tf_op jit(solution)/shard_map/reduce_scatter | solution.py:309
  727.2 33.4 %copy-start.7 = (f32[8,256,128]{2,1,0:T(8,128)S(1)}, f32[8,256,128]{2,1,0:T(8,128)}, u32[]{:S(2)}) copy-start(f32[8,256,128]{2,1,0:T(8,128)} %reduce-scatter.7.cloned.1.call-done) | copy-start | bytes 3145732
  727.2 70.5 %all-gather.13.cloned.1.call-start = ((), (), s32[]{:S(2)}) async-start(), calls=%async_computation.20 | async-start | bytes 2621440 | tf_op jit(solution)/shard_map/all_gather | solution.py:324
  760.5 74.3 %all-gather.15.cloned.1.call-start = ((), (), s32[]{:S(2)}) async-start(), calls=%async_computation.21 | async-start | bytes 2621440 | tf_op jit(solution)/shard_map/all_gather | solution.py:324
  837.6 10.0 %copy-start.1 = (f32[1,256,256]{2,1,0:T(8,128)S(1)}, f32[1,256,256]{2,1,0:T(8,128)}, u32[]{:S(2)}) copy-start(f32[1,256,256]{2,1,0:T(8,128)} %param.11) | copy-start | bytes 786436
Sparse Core Ops, SparseCore 0:
  130.5 51.5 reduce-scatter.4
  185.9 52.6 reduce-scatter.6
  276.3 52.7 all-gather.8
  358.7 53.1 all-gather.10
  664.3 33.1 reduce-scatter.10
  727.3 33.1 reduce-scatter.8
  762.3 35.2 all-gather.12
  799.5 35.2 all-gather.14
